TPU v7x, 256 devices: a whole 4x4x8 slice. The times are simulated.
256 devices in a mesh: blk: 64 (over z, x, core), rep: 4 (over y).
Axes of the slice: x: 4, y: 4, z: 8, core: 2. Of those that a mesh axis runs over, the one named last changes fastest.
Arguments:
- embeddings: float32 [12288, 256], P('blk'), may hold values from -3 to 3
- partner: int32 [12288], P('blk'), may hold values from 0 to 12287, as said below
Outputs:
- view_loss: float32 [12288], P('blk')
- grad: float32 [12288, 256], P('blk')
Inputs may be any that keep to these rules, and one draw needn't show every extreme that they name: A view's partner is another view of the same block of 192 views, and the partner's partner is the view itself.
All inputs are finite; a program needn't handle non-finite values.
Results may differ from a plain program's by a relative error of at most 0.0003.
Values sent between devices are 32-bit elements; how exact they have to be, the bound alone decides.
A program may use at most 128 MiB of HBM per device.

v0:
```python
import jax
import jax.numpy as jnp
from jax import lax
from jax.sharding import PartitionSpec as P

INV_TEMP = 10.0


def add_rows(total, start, extra):
    current = lax.dynamic_slice_in_dim(total, start, extra.shape[0], 0)
    return lax.dynamic_update_slice_in_dim(total, current + extra, start, 0)


def body(embeddings, partner):
    rows, width = embeddings.shape
    blocks = lax.axis_size("blk")
    mine = lax.axis_index("blk")
    groups = lax.axis_size("rep")
    member = lax.axis_index("rep")
    norms = jnp.sqrt(jnp.sum(embeddings * embeddings, axis=1, keepdims=True) + 1e-12)
    unit = embeddings / norms
    every = lax.all_gather(unit, "blk", axis=0, tiled=True)
    local = jnp.arange(rows, dtype=jnp.int32)
    self_mask = (local[:, None] == local[None, :]).astype(jnp.float32)
    count = blocks // groups

    def pick(slot):
        distance = member + groups * slot
        other = mine + distance
        valid = other < blocks
        return (jnp.minimum(other, blocks - 1), valid)

    def tile_parts(other):
        piece = lax.dynamic_slice_in_dim(every, other * rows, rows, 0)
        same = (other == mine).astype(jnp.float32)
        keep = 1.0 - same * self_mask
        return (piece, keep, 1.0 - same)

    def gram(piece):
        return (
            jnp.dot(
                unit, piece.T, precision=lax.Precision.HIGHEST, preferred_element_type=jnp.float32
            )
            * INV_TEMP
        )

    def forward_slot(slot, carry):
        other, valid = pick(slot)

        def forward_work(carry):
            sums, kept = carry
            piece, keep, apart = tile_parts(other)
            scores = gram(piece)
            weights = jnp.exp(scores - INV_TEMP) * keep
            sums = add_rows(sums, mine * rows, jnp.sum(weights, axis=1))
            sums = add_rows(sums, other * rows, jnp.sum(weights, axis=0) * apart)
            return (sums, kept)

        return lax.cond(valid, forward_work, lambda c: c, carry)

    kept_init = jnp.zeros((1, 1, 1), jnp.float32)
    sums, kept = lax.fori_loop(
        0, count, forward_slot, (jnp.zeros((blocks * rows,), jnp.float32), kept_init)
    )
    share = lax.psum_scatter(sums, "blk", scatter_dimension=0, tiled=True)
    totals = lax.psum(share, "rep")
    lse = jnp.log(totals) + INV_TEMP
    lse_every = lax.all_gather(lse, "blk", axis=0, tiled=True)

    def backward_slot(slot, pulls):
        other, valid = pick(slot)

        def backward_work(pulls):
            piece, keep, apart = tile_parts(other)
            scores = gram(piece)
            lse_other = lax.dynamic_slice_in_dim(lse_every, other * rows, rows, 0)
            both = (jnp.exp(scores - lse[:, None]) + jnp.exp(scores - lse_other[None, :])) * keep
            near = jnp.dot(
                both, piece, precision=lax.Precision.HIGHEST, preferred_element_type=jnp.float32
            )
            far = lax.dot_general(
                both,
                unit,
                (((0,), (0,)), ((), ())),
                precision=lax.Precision.HIGHEST,
                preferred_element_type=jnp.float32,
            )
            pulls = add_rows(pulls, mine * rows, near)
            return add_rows(pulls, other * rows, far * apart)

        return lax.cond(valid, backward_work, lambda p: p, pulls)

    pulls = lax.fori_loop(0, count, backward_slot, jnp.zeros((blocks * rows, width), jnp.float32))
    pull_share = lax.psum_scatter(pulls, "blk", scatter_dimension=0, tiled=True)
    pull = lax.psum(pull_share, "rep")
    mates = unit[partner - mine * rows]
    view_loss = lse - INV_TEMP * jnp.sum(unit * mates, axis=1)
    grad_unit = INV_TEMP * (pull - 2.0 * mates)
    grad = (grad_unit - unit * jnp.sum(unit * grad_unit, axis=1, keepdims=True)) / norms
    return (view_loss, grad)


def solution(mesh):
    return jax.shard_map(
        body,
        mesh=mesh,
        in_specs=(P("blk", None), P("blk")),
        out_specs=(P("blk"), P("blk", None)),
        check_vma=False,
    )
```

profile of v0, /device:TPU:1, one launch (start us, length us, event | category | flops | bytes accessed | tf_op | source)
XLA Modules:
  0.0 942.2 jit_solution(10421335674066473831)
XLA Ops:
  12.7 92.8 %all-gather.2.cloned.1.call-done = f32[12288,256]{1,0:T(8,128)} async-done(((f32[192,256]{1,0:T(8,128)}), f32[12288,256]{1,0:T(8,128)}) %all-gather.2.cloned.1.call-update) | async-done | bytes 12582928 | tf_op jit(solution)/shard_map/all_gather | solution.py:22
  105.5 30.6 %while.34 = (s32[]{:T(128)}, f32[12288]{0:T(1024)S(1)}, s32[]{:T(128)}, s32[]{:T(128)}, f32[12288,256]{1,0:T(8,128)}, /*index=5*/f32[192,256]{1,0:T(8,128)}, s32[]{:T(128)}, s32[]{:T(128)}, s32[]{:T(128)}) while((s32[]{:T(128)}, f32[12288]{0:T(1024)S(1)}, s32[]{:T(128)}, s32[]{:T(128)}, f32[12288,256]{1,0:T(8,128)}, ...), condition=%wide.region_6.0_spmd.clone, body=%wide.region_1.0_spmd.clone.sunk | while | flops 113578192 | bytes 696157 | solution.py:62
  136.1 241.1 %all-reduce.1 = f32[12288]{0:T(1024)S(1)} all-reduce(f32[12288]{0:T(1024)S(1)} %get-tuple-element.370), channel_id=2, replica_groups=mesh['blk'=64,'rep'=4] {'blk'}, use_global_device_ids=true, to_apply=%region_7.0.clone | all-reduce | flops 12288 | bytes 98304
  377.3 8.4 psum.14
  385.8 247.9 %all-reduce = f32[12288]{0:T(1024)S(1)} all-reduce(f32[12288]{0:T(1024)S(1)} %get-tuple-element.436), channel_id=1, replica_groups=mesh['blk'=64,'rep'=4] {'blk'}, use_global_device_ids=true, to_apply=%add | all-reduce | flops 12288 | bytes 98304
  638.5 90.7 %while.35 = (s32[]{:T(128)}, f32[12288,256]{1,0:T(8,128)}, s32[]{:T(128)}, s32[]{:T(128)}, f32[12288,256]{1,0:T(8,128)}, /*index=5*/f32[192,256]{1,0:T(8,128)S(1...) while((s32[]{:T(128)}, f32[12288,256]{1,0:T(8,128)}, ...), condition=%wide.region_13.0_spmd.clone, body=%wide.region_10.13_spmd.clone.sunk | while | flops 340217856 | bytes 2313605 | solution.py:93
  638.5 5.7 conditional.7
  644.2 5.7 conditional.7
  649.9 5.6 conditional.7
  655.5 5.6 conditional.7
  661.2 5.6 conditional.7
  666.9 5.6 conditional.7
  672.5 5.6 conditional.7
  678.2 5.6 conditional.7
  683.8 5.6 conditional.7
  689.5 5.7 conditional.7
  695.2 5.6 conditional.7
  700.8 5.7 conditional.7
  706.5 5.7 conditional.7
  712.2 5.7 conditional.7
  717.9 5.6 conditional.7
  723.5 5.6 conditional.7
  729.2 153.8 %reduce-scatter.2.cloned.1.call-done = f32[192,256]{1,0:T(8,128)} async-done(((f32[12288,256]{1,0:T(8,128)}), f32[192,256]{1,0:T(8,128)}) %reduce-scatter.2.cloned.1.call-update) | async-done | bytes 196624 | tf_op jit(solution)/shard_map/reduce_scatter | solution.py:94
  884.0 48.2 %all-reduce.4.cloned.1.call-done = f32[192,256]{1,0:T(8,128)} async-done(((f32[192,256]{1,0:T(8,128)}), f32[192,256]{1,0:T(8,128)}) %all-reduce.4.cloned.1.call-update) | async-done | bytes 196624 | tf_op jit(solution)/shard_map/psum | solution.py:95
  (187 shorter events, 163.7 us)
Async XLA Ops:
  7.2 98.4 %all-gather.2.cloned.1.call-start = ((), (), s32[]{:S(2)}) async-start(), calls=%async_computation.1 | async-start | bytes 12779520 | tf_op jit(solution)/shard_map/all_gather | solution.py:22
  10.0 873.1 %reduce-scatter.2.cloned.1.call-start = ((), (), s32[]{:S(2)}) async-start(), calls=%async_computation.2 | async-start | bytes 12779520 | tf_op jit(solution)/shard_map/reduce_scatter | solution.py:94
  136.1 502.4 %copy-start = (f32[192,256]{1,0:T(8,128)S(1)}, f32[192,256]{1,0:T(8,128)}, u32[]{:S(2)}) copy-start(f32[192,256]{1,0:T(8,128)} %get-tuple-element.593) | copy-start | bytes 589828
  638.5 244.6 %copy-start.2 = (s32[192]{0:T(256)S(1)}, s32[192]{0:T(256)}, u32[]{:S(2)}) copy-start(s32[192]{0:T(256)} %param.11) | copy-start | bytes 2308
  638.5 293.7 %copy-start.1 = (f32[192,256]{1,0:T(8,128)S(1)}, f32[192,256]{1,0:T(8,128)}, u32[]{:S(2)}) copy-start(f32[192,256]{1,0:T(8,128)} %param.10) | copy-start | bytes 589828
  729.2 203.0 %all-reduce.4.cloned.1.call-start = ((), (), s32[]{:S(2)}) async-start(), calls=%async_computation.3 | async-start | bytes 393216 | tf_op jit(solution)/shard_map/psum | solution.py:95
Sparse Core Ops, SparseCore 0:
  11.3 94.1 all-gather.1
  729.3 153.7 reduce-scatter.1
  885.5 46.6 all-reduce.3
where the time goes:
time: 945 us; the launch traced here: 942 us
  blocking collectives  497 us (53%)
  waiting for transfers between devices  295 us (31%)
  matrix products  112 us (12%)
  between operations  15 us (2%)
  other arithmetic  12.5 us (1%)
    unnamed x2, blocking collectives  489 us
    reduce_scatter x1, waiting for transfers between devices, body(): pull_share = lax.psum_scatter(pulls, 'blk', scatter_dimension=0, tiled=True)  154 us
    all_gather x1, waiting for transfers between devices, body(): every = lax.all_gather(unit, 'blk', axis=0, tiled=True)  92.8 us
    psum x1, waiting for transfers between devices, body(): pull = lax.psum(pull_share, 'rep')  48.2 us
    dot_general x32, matrix products, gram(): jnp.dot(unit, piece.T, precision=lax.Precision.HIGHEST, preferred_element...  45 us
    dot_general x16, matrix products, backward_work(): jnp.dot(both, piece, precision=lax.Precision.HIGHEST, preferred_element_t...  36.6 us
    dot_general x16, matrix products, backward_work(): lax.dot_general(both, unit, (((0,), (0,)), ((), ())), precision=lax.Preci...  30.8 us
  transfers between devices with their start and end apart: 3, of which 3 were waited for; matrix products, arithmetic and copies ran while one was open for 0% of the time, Pallas kernels for 0%

commit v1 on v0

v1 whole, which is shorter than its diff:
```python
import jax
import jax.numpy as jnp
from jax import lax
from jax.experimental import pallas as pl
from jax.experimental.pallas import tpu as pltpu
from jax.sharding import PartitionSpec as P

MESH = pl.DeviceIdType.MESH
F32 = jnp.float32
BF16 = jnp.bfloat16
HIGHEST = lax.Precision.HIGHEST
INV_TEMP = 10.0
ROWS = 192
WIDTH = 256
XS, YS, ZS, CORES = 4, 4, 8, 2
CHUNKS = 2
CHUNK = ROWS // CHUNKS
SHARE = ROWS // YS


def dot_nn(a, b, precision=None):
    return lax.dot_general(
        a, b, (((1,), (0,)), ((), ())), precision=precision, preferred_element_type=F32
    )


def dot_nt(a, b, precision=None):
    return lax.dot_general(
        a, b, (((1,), (1,)), ((), ())), precision=precision, preferred_element_type=F32
    )


def split(value):
    high = value.astype(BF16)
    return high, (value - high.astype(F32)).astype(BF16)


def kernel(
    emb_ref,
    partner_ref,
    loss_ref,
    grad_ref,
    ui,
    ui_hi,
    ui_lo,
    norms,
    mates,
    uj,
    uj_hi,
    uj_lo,
    weights,
    acc,
    sums,
    inverse,
    inverse_rows,
    inverse_cols,
    pull_out,
    pull_in,
    pull_own,
    shares,
    gather_send,
    gather_recv,
    own_send,
    sums_send,
    sums_recv,
    inv_send,
    inv_recv,
    sib_send,
    sib_recv,
    share_send,
    share_recv,
    grad_send,
    grad_recv,
):
    blk = lax.axis_index("blk")
    y = lax.axis_index("rep")
    core = lax.rem(blk, CORES)
    x = lax.rem(lax.div(blk, CORES), XS)
    z = lax.div(blk, CORES * XS)

    def device(dx=0, dy=0, dz=0, dc=0):
        there = lax.rem(z + (dz % ZS), ZS) * XS + lax.rem(x + (dx % XS), XS)
        return (there * CORES + lax.rem(core + dc, CORES), lax.rem(y + (dy % YS), YS))

    is_a = core == 0
    is_b = core == 1
    offset = lax.rem(z + ZS - y, 4)
    a_source = jnp.logical_and(is_a, offset == 0)
    b_source = jnp.logical_and(is_b, x == y)
    is_source = jnp.logical_or(a_source, b_source)
    own_rows = pl.ds(pl.multiple_of(core * ROWS, ROWS), ROWS)
    sib_rows = pl.ds(pl.multiple_of((1 - core) * ROWS, ROWS), ROWS)

    group = [(dy, dc) for dc in range(CORES) for dy in range(YS) if (dy, dc) != (0, 0)]
    near = [device(dy=dy, dc=dc) for dy, dc in group]
    near += [device(dx=d) for d in (1, 2, 3)] + [device(dz=d) for d in (1, 7)]
    barrier = pltpu.get_barrier_semaphore()
    for peer in near:
        pl.semaphore_signal(barrier, inc=1, device_id=peer, device_id_type=MESH)

    emb = emb_ref[...]
    norm = jnp.sqrt(jnp.sum(emb * emb, axis=1, keepdims=True) + 1e-12)
    unit = emb / norm
    norms[...] = norm
    ui[own_rows, :] = unit

    @pl.when(is_source)
    def _():
        uj[0] = unit

    pl.semaphore_wait(barrier, len(near))

    sent = []

    def send(cond, src, dst, send_sem, recv_sem, peer):
        copy = pltpu.make_async_remote_copy(
            src_ref=src,
            dst_ref=dst,
            send_sem=send_sem,
            recv_sem=recv_sem,
            device_id=peer,
            device_id_type=MESH,
        )
        if cond is None:
            copy.start()
        else:
            pl.when(cond)(copy.start)
        sent.append((cond, copy))

    def arrived(dst, recv_sem):
        pltpu.make_async_remote_copy(
            src_ref=dst,
            dst_ref=dst,
            send_sem=recv_sem,
            recv_sem=recv_sem,
            device_id=device(dc=1),
            device_id_type=MESH,
        ).wait_recv()

    def part(slot, h):
        return uj.at[slot, pl.ds(h * CHUNK, CHUNK)]

    def forward(cond, slot, to_slot, h, lane, peer):
        send(
            cond,
            part(slot, h),
            part(to_slot, h),
            gather_send.at[slot, h, lane],
            gather_recv.at[to_slot, h],
            peer,
        )

    def await_part(cond, slot, h):
        def wait():
            arrived(part(slot, h), gather_recv.at[slot, h])

        pl.when(cond)(wait)

    both = range(CHUNKS)
    last_half = CHUNKS // 2

    send(None, ui.at[own_rows], ui.at[own_rows], own_send, sib_recv.at[1], device(dc=1))

    def x_spread(cond, slot, h):
        forward(cond, slot, slot + 1, h, 2, device(dx=1))
        forward(cond, slot, slot + 2, h, 3, device(dx=-1))

    a_other = jnp.logical_and(is_a, offset != 0)
    b_other = jnp.logical_and(is_b, x != y)
    near_up = jnp.logical_and(is_a, jnp.logical_or(offset == 1, offset == 2))
    near_down = jnp.logical_and(is_a, offset == 3)
    near_to = jnp.where(offset >= 2, 3, 0)
    for h in both:
        forward(a_source, 0, 0, h, 0, device(dz=1))
        forward(a_source, 0, 0, h, 1, device(dz=-1))
        x_spread(a_source, 0, h)
        forward(b_source, 0, 0, h, 2, device(dx=2))
        forward(b_source, 0, 0, h, 3, device(dx=1))
        forward(b_source, 0, 0, h, 4, device(dx=-1))
        forward(b_source, 0, 1, h, 0, device(dz=1))
        forward(b_source, 0, 2, h, 1, device(dz=-1))
    for h in both:
        await_part(jnp.logical_not(is_source), 0, h)
        forward(near_up, 0, near_to, h, 0, device(dz=1))
        forward(near_down, 0, near_to, h, 1, device(dz=-1))
        x_spread(a_other, 0, h)
        forward(b_other, 0, 1, h, 0, device(dz=1))
        forward(b_other, 0, 2, h, 1, device(dz=-1))

    def far_column(cond):
        far_up = jnp.logical_and(cond, offset == 3)
        far_down = jnp.logical_and(cond, jnp.logical_or(offset == 1, offset == 2))
        for h in both:
            await_part(cond, 3, h)
            if h < last_half:
                forward(far_up, 3, 3, h, 0, device(dz=1))
                forward(
                    jnp.logical_and(cond, offset == 2), 3, 3, h, 1, device(dz=-1)
                )
            else:
                forward(far_down, 3, 3, h, 1, device(dz=-1))
            x_spread(cond, 3, h)

    far_column(jnp.logical_and(is_a, offset == 2))

    def a_pair(left, right, to):
        for h in both:
            await_part(is_a, left, h)
            if h < last_half:
                forward(is_a, left, to, h, 2, device(dx=1))
            await_part(is_a, right, h)
            if h >= last_half:
                forward(is_a, right, to, h, 3, device(dx=-1))

    def b_pair(up, down):
        for h in both:
            await_part(is_b, up, h)
            if up < 5:
                forward(is_b, up, up + 2, h, 0, device(dz=1))
            elif h < last_half:
                forward(is_b, up, 7, h, 0, device(dz=1))
            await_part(is_b, down, h)
            if down < 6:
                forward(is_b, down, down + 2, h, 1, device(dz=-1))
            elif h >= last_half:
                forward(is_b, down, 7, h, 1, device(dz=-1))

    def scores(slot):
        high, low = split(uj[slot])
        uj_hi[slot] = high
        uj_lo[slot] = low
        left, left_low = ui_hi[...], ui_lo[...]
        score = dot_nt(left, high) + dot_nt(left_low, high) + dot_nt(left, low)
        weight = jnp.exp(score * INV_TEMP - INV_TEMP)
        if slot == 0:
            row = lax.broadcasted_iota(jnp.int32, weight.shape, 0)
            col = lax.broadcasted_iota(jnp.int32, weight.shape, 1)
            start = jnp.where(is_source, core * ROWS, 2 * CORES * ROWS)
            weight = jnp.where(row == col + start, 0.0, weight)
            acc[...] = weight
        else:
            acc[...] += weight
        weights[slot] = weight

    arrived(ui.at[sib_rows], sib_recv.at[1])
    high, low = split(ui[...])
    ui_hi[...] = high
    ui_lo[...] = low
    scores(0)
    a_pair(1, 2, 6)
    b_pair(1, 2)
    scores(1)
    scores(2)
    far_column(jnp.logical_and(is_a, offset != 2))
    b_pair(3, 4)
    scores(3)
    a_pair(4, 5, 7)
    scores(4)
    b_pair(5, 6)
    scores(5)
    for h in both:
        await_part(is_a, 6, h)
    scores(6)
    for h in both:
        await_part(is_a, 7, h)
        await_part(is_b, 7, h)
    scores(7)

    mine = y * CORES + core
    ones = jnp.ones((8, ROWS), F32)
    for c in range(CORES):
        sums[mine, c] = dot_nt(ones, acc[c * ROWS : (c + 1) * ROWS, :], HIGHEST)[0:1]
    for i, (dy, dc) in enumerate(group):
        send(
            None,
            sums.at[mine],
            sums.at[mine],
            sums_send.at[i],
            sums_recv.at[mine],
            device(dy=dy, dc=dc),
        )
    unit = ui[own_rows, :]
    node = lax.broadcasted_iota(jnp.int32, (ROWS, ROWS), 0)
    pairing = (node == partner_ref[...]).astype(F32)
    mate = dot_nn(pairing, unit, HIGHEST)
    mates[...] = mate
    pair_score = dot_nt(jnp.ones((8, WIDTH), F32), unit * mate, HIGHEST)[0:1]
    for dy, dc in group:
        other = lax.rem(y + dy, YS) * CORES + lax.rem(core + dc, CORES)
        arrived(sums.at[other], sums_recv.at[other])
    total = sums[0]
    for i in range(1, YS * CORES):
        total = total + sums[i]
    inverse[...] = 1.0 / total

    plane = jnp.where(is_a, lax.rem(z, 4), x)
    shift = lax.rem(2 + y + YS - plane, YS)
    column = jnp.where(shift == 2, 3, jnp.where(shift == 3, 2, shift))
    for dz in range(ZS):
        far_slot = jnp.where(column == 3, 7, column + 3)
        near_slot = jnp.where(column == 3, 6, column)
        a_slot = near_slot if dz in (0, 1, 2, 7) else far_slot
        b_slot = (0, 1, 3, 5, 7, 6, 4, 2)[dz]
        slot = jnp.where(is_a, a_slot, b_slot)
        there = lax.rem(z + dz, ZS) * XS + lax.rem(x + shift, XS)
        send(
            None,
            inverse.at[core],
            inverse_cols.at[slot],
            inv_send.at[dz],
            inv_recv.at[slot],
            (there * CORES + core, plane),
        )
    loss_ref[...] = jnp.log(jnp.where(is_a, total[0], total[1])) + INV_TEMP - INV_TEMP * pair_score
    same = lax.broadcasted_iota(jnp.int32, (ROWS, ROWS), 1) == node
    for c in range(CORES):
        column_sum = jnp.sum(jnp.where(same, inverse[c], 0.0), axis=1, keepdims=True)
        inverse_rows[c * ROWS : (c + 1) * ROWS, :] = jnp.broadcast_to(column_sum, (ROWS, ROWS))
    for slot in range(8):
        arrived(inverse_cols.at[slot], inv_recv.at[slot])

    def pulls(rows):
        total = jnp.zeros((ROWS, WIDTH), F32)
        for slot in range(8):
            both = weights[slot, rows, :] * (inverse_rows[rows, :] + inverse_cols[slot])
            high, low = split(both)
            total = total + dot_nn(high, uj_hi[slot])
            total = total + dot_nn(low, uj_hi[slot])
            total = total + dot_nn(high, uj_lo[slot])
        return total

    pull_out[...] = pulls(sib_rows)
    send(None, pull_out, pull_in, sib_send, sib_recv.at[0], device(dc=1))
    own = pulls(own_rows)
    arrived(pull_in, sib_recv.at[0])
    pull_own[...] = own + pull_in[...]
    for dy in range(1, YS):
        rows = pl.ds(pl.multiple_of(lax.rem(y + dy, YS) * SHARE, SHARE), SHARE)
        send(
            None,
            pull_own.at[rows],
            shares.at[dy - 1],
            share_send.at[dy - 1],
            share_recv.at[dy - 1],
            device(dy=dy),
        )
    for dy in range(1, YS):
        arrived(shares.at[dy - 1], share_recv.at[dy - 1])
    rows = pl.ds(pl.multiple_of(y * SHARE, SHARE), SHARE)
    pull = pull_own[rows, :] + shares[0] + shares[1] + shares[2]
    unit = ui[pl.ds(pl.multiple_of(core * ROWS + y * SHARE, SHARE), SHARE), :]
    grad_unit = INV_TEMP * (pull - 2.0 * mates[rows, :])
    along = jnp.sum(unit * grad_unit, axis=1, keepdims=True)
    grad_ref[rows, :] = (grad_unit - unit * along) / norms[rows, :]
    for dy in range(1, YS):
        send(
            None,
            grad_ref.at[rows],
            grad_ref.at[rows],
            grad_send.at[dy - 1],
            grad_recv.at[dy - 1],
            device(dy=dy),
        )
    for dy in range(1, YS):
        from_rows = pl.ds(pl.multiple_of(lax.rem(y + YS - dy, YS) * SHARE, SHARE), SHARE)
        arrived(grad_ref.at[from_rows], grad_recv.at[dy - 1])
    for cond, copy in sent:
        if cond is None:
            copy.wait_send()
        else:
            pl.when(cond)(copy.wait_send)


def body(embeddings, partner):
    local = (partner - lax.axis_index("blk") * ROWS).reshape(1, ROWS)
    vmem = pl.BlockSpec(memory_space=pltpu.VMEM)
    dma = pltpu.SemaphoreType.DMA
    loss, grad = pl.pallas_call(
        kernel,
        out_shape=(
            jax.ShapeDtypeStruct((1, ROWS), F32),
            jax.ShapeDtypeStruct((ROWS, WIDTH), F32),
        ),
        in_specs=[vmem, vmem],
        out_specs=(vmem, vmem),
        scratch_shapes=[
            pltpu.VMEM((CORES * ROWS, WIDTH), F32),
            pltpu.VMEM((CORES * ROWS, WIDTH), BF16),
            pltpu.VMEM((CORES * ROWS, WIDTH), BF16),
            pltpu.VMEM((ROWS, 1), F32),
            pltpu.VMEM((ROWS, WIDTH), F32),
            pltpu.VMEM((8, ROWS, WIDTH), F32),
            pltpu.VMEM((8, ROWS, WIDTH), BF16),
            pltpu.VMEM((8, ROWS, WIDTH), BF16),
            pltpu.VMEM((8, CORES * ROWS, ROWS), F32),
            pltpu.VMEM((CORES * ROWS, ROWS), F32),
            pltpu.VMEM((8, CORES, 1, ROWS), F32),
            pltpu.VMEM((CORES, 1, ROWS), F32),
            pltpu.VMEM((CORES * ROWS, ROWS), F32),
            pltpu.VMEM((8, 1, ROWS), F32),
            pltpu.VMEM((ROWS, WIDTH), F32),
            pltpu.VMEM((ROWS, WIDTH), F32),
            pltpu.VMEM((ROWS, WIDTH), F32),
            pltpu.VMEM((YS - 1, SHARE, WIDTH), F32),
            dma((8, CHUNKS, 5)),
            dma((8, CHUNKS)),
            dma,
            dma((7,)),
            dma((8,)),
            dma((8,)),
            dma((8,)),
            dma,
            dma((2,)),
            dma((3,)),
            dma((3,)),
            dma((3,)),
            dma((3,)),
        ],
        compiler_params=pltpu.CompilerParams(
            collective_id=0, has_side_effects=True, vmem_limit_bytes=48 * 2**20
        ),
    )(embeddings, local)
    return loss.reshape(ROWS), grad


def solution(mesh):
    return jax.shard_map(
        body,
        mesh=mesh,
        in_specs=(P("blk", None), P("blk")),
        out_specs=(P("blk"), P("blk", None)),
        check_vma=False,
    )
```

time: 945 us -> 63.6 us (0.07)
  blocking collectives: 497 us -> 0 us
  waiting for transfers between devices: 295 us -> 0 us
  matrix products: 112 us -> 0 us
  Pallas kernels: 0 us -> 59.9 us
  between operations: 15 us -> 0.65 us
  other arithmetic: 12.5 us -> 0.01 us
    unnamed x2 -> x0, blocking collectives: 489 us -> none
    reduce_scatter x1 -> x0, waiting for transfers between devices: 154 us -> none  [body(): pull_share = lax.psum_scatter(pulls, 'blk', scatter_dimension=0, tiled=True)]
    dot_general x64 -> x0, matrix products: 112 us -> none  [the longest x32 45 us: gram(): jnp.dot(unit, piece.T, precision=lax.Precision.HIGHEST, preferred_element...]
    all_gather x1 -> x0, waiting for transfers between devices: 92.8 us -> none  [body(): every = lax.all_gather(unit, 'blk', axis=0, tiled=True)]
    pallas_call x0 -> x1, Pallas kernels: none -> 59.9 us  [body(): pl.pallas_call(kernel, out_shape=(jax.ShapeDtypeStruct((1, ROWS), F32), j...]
    psum x1 -> x0, waiting for transfers between devices: 48.2 us -> none  [body(): pull = lax.psum(pull_share, 'rep')]
  transfers between devices with their start and end apart: 3 -> 0, of which waited for: 3 -> 0; matrix products, arithmetic and copies ran while one was open for 0% -> 0% of each run, Pallas kernels for 0% -> 0%
where the time goes in v1:
time: 63.6 us; the launch traced here: 63.4 us
  Pallas kernels  59.9 us (94%)
  local copies, waits for them, and re-layouts  2.84 us (4%)
  between operations  0.65 us (1%)
    pallas_call x1, Pallas kernels, body(): pl.pallas_call(kernel, out_shape=(jax.ShapeDtypeStruct((1, ROWS), F32), j...  59.9 us
    unnamed x6, local copies, waits for them, and re-layouts  2.84 us

profile of v1, /device:TPU:1, one launch (start us, length us, event | category | flops | bytes accessed | tf_op | source)
XLA Modules:
  0.0 63.4 jit_solution(8069449733641294590)
XLA Ops:
  0.6 0.0 copy-start.1
  0.6 0.7 %copy-done.1 = s32[192]{0:T(256)S(1)} copy-done((s32[192]{0:T(256)S(1)}, s32[192]{0:T(256)}, u32[]{:S(2)}) %copy-start.1) | copy-done | bytes 792
  1.3 0.0 copy-start
  1.3 0.9 %copy-done = f32[192,256]{1,0:T(8,128)S(1)} copy-done((f32[192,256]{1,0:T(8,128)S(1)}, f32[192,256]{1,0:T(8,128)}, u32[]{:S(2)}) %copy-start) | copy-done | bytes 196632
  2.2 59.9 %shard_map.41 = (f32[1,192]{1,0:T(1,128)S(1)}, f32[192,256]{1,0:T(8,128)S(1)}) custom-call(f32[192,256]{1,0:T(8,128)S(1)} %copy-done, s32[1,192]{1,0:T(1,128)S(1)} %bitcast.2), custom_call_target="tpu_custom_call" | custom-call | tf_op jit(solution)/shard_map/pallas_call | solution.py:378
  62.2 0.6 copy.6
  62.8 0.7 %copy.7 = f32[192,256]{1,0:T(8,128)} copy(f32[192,256]{1,0:T(8,128)S(1)} %get-tuple-element.9) | data formatting | bytes 393216
  (1 shorter events, 0.0 us)
Async XLA Ops:
  0.6 0.7 %copy-start.1 = (s32[192]{0:T(256)S(1)}, s32[192]{0:T(256)}, u32[]{:S(2)}) copy-start(s32[192]{0:T(256)} %param.3) | copy-start | bytes 2308
  1.3 0.9 %copy-start = (f32[192,256]{1,0:T(8,128)S(1)}, f32[192,256]{1,0:T(8,128)}, u32[]{:S(2)}) copy-start(f32[192,256]{1,0:T(8,128)} %emb_ref.1) | copy-start | bytes 589828

commit v2 on v1

v2 whole, which is shorter than its diff:
```python
import jax
import jax.numpy as jnp
from jax import lax
from jax.experimental import pallas as pl
from jax.experimental.pallas import tpu as pltpu
from jax.sharding import PartitionSpec as P

MESH = pl.DeviceIdType.MESH
F32 = jnp.float32
BF16 = jnp.bfloat16
HIGHEST = lax.Precision.HIGHEST
INV_TEMP = 10.0
ROWS = 192
WIDTH = 256
XS, YS, ZS, CORES = 4, 4, 8, 2
HALF = ROWS // 2
SHARE = ROWS // YS
ALL = 4 * ROWS


def dot_nn(a, b, precision=None):
    return lax.dot_general(
        a, b, (((1,), (0,)), ((), ())), precision=precision, preferred_element_type=F32
    )


def dot_nt(a, b, precision=None):
    return lax.dot_general(
        a, b, (((1,), (1,)), ((), ())), precision=precision, preferred_element_type=F32
    )


def split(value):
    high = value.astype(BF16)
    return high, (value - high.astype(F32)).astype(BF16)


def kernel(
    emb_hbm,
    partner_hbm,
    loss_ref,
    grad_ref,
    emb_ref,
    partner_ref,
    ui,
    ui_hi,
    ui_lo,
    norms,
    mates,
    uj,
    uj_hi,
    uj_lo,
    weights,
    acc,
    sums,
    inverse,
    inverse_rows,
    inverse_cols,
    pull_out,
    pull_in,
    pull_own,
    shares,
    local_sem,
    z_send,
    z_recv,
    x_send,
    x_recv,
    row_send,
    row_recv,
    sums_send,
    sums_recv,
    inv_send,
    inv_recv,
    sib_send,
    sib_recv,
    share_send,
    share_recv,
    grad_send,
    grad_recv,
):
    blk = lax.axis_index("blk")
    y = lax.axis_index("rep")
    core = lax.rem(blk, CORES)
    x = lax.rem(lax.div(blk, CORES), XS)
    z = lax.div(blk, CORES * XS)
    odd = lax.rem(z, 2)
    z_pair = z + 1 - 2 * odd

    def device(dx=0, dy=0, to_z=None, dc=0):
        there = (z if to_z is None else to_z) * XS + lax.rem(x + (dx % XS), XS)
        return (there * CORES + lax.rem(core + dc, CORES), lax.rem(y + (dy % YS), YS))

    steps = (y, YS - 1 - y)
    z_to = [
        lax.rem(z + ZS + jnp.where(lax.rem(z + k, 2) == 0, k, -k), ZS) for k in steps
    ]
    z_from = [lax.rem(z + ZS + jnp.where(odd == 0, -k, k), ZS) for k in steps]

    embedding_copy = pltpu.make_async_copy(emb_hbm, emb_ref, local_sem.at[0])
    partner_copy = pltpu.make_async_copy(partner_hbm, partner_ref, local_sem.at[1])
    embedding_copy.start()
    partner_copy.start()

    group = [
        (dy, db, dc)
        for dy in range(YS)
        for db in range(2)
        for dc in range(CORES)
        if (dy, db, dc) != (0, 0, 0)
    ]
    near = [device(dy=dy, to_z=z_pair if db else z, dc=dc) for dy, db, dc in group]
    near += [device(dx=d) for d in (1, 2, 3)]
    barrier = pltpu.get_barrier_semaphore()
    for peer in near:
        pl.semaphore_signal(barrier, inc=1, device_id=peer, device_id_type=MESH)
    for k, source in zip(steps, z_from):

        @pl.when(k != 0)
        def _():
            pl.semaphore_signal(
                barrier, inc=1, device_id=device(to_z=source), device_id_type=MESH
            )

    own_at = (core * 2 + odd) * ROWS
    own_rows = pl.ds(pl.multiple_of(own_at, ROWS), ROWS)
    sib_rows = pl.ds(pl.multiple_of(((1 - core) * 2 + odd) * ROWS, ROWS), ROWS)
    pair_rows = pl.ds(pl.multiple_of((core * 2 + 1 - odd) * ROWS, ROWS), ROWS)
    last_rows = pl.ds(pl.multiple_of(((1 - core) * 2 + 1 - odd) * ROWS, ROWS), ROWS)

    embedding_copy.wait()
    emb = emb_ref[...]
    norm = jnp.sqrt(jnp.sum(emb * emb, axis=1, keepdims=True) + 1e-12)
    unit = emb / norm
    norms[...] = norm
    ui[own_rows, :] = unit
    for h, k in enumerate(steps):

        @pl.when(k == 0)
        def _():
            uj[0, h * HALF : (h + 1) * HALF] = unit[h * HALF : (h + 1) * HALF]

    pl.semaphore_wait(
        barrier, len(near) + 2 - jnp.where(jnp.logical_or(y == 0, y == YS - 1), 1, 0)
    )

    sent = []

    def send(cond, src, dst, send_sem, recv_sem, peer):
        copy = pltpu.make_async_remote_copy(
            src_ref=src,
            dst_ref=dst,
            send_sem=send_sem,
            recv_sem=recv_sem,
            device_id=peer,
            device_id_type=MESH,
        )
        if cond is None:
            copy.start()
        else:
            pl.when(cond)(copy.start)
        sent.append((cond, copy))

    def arrived(dst, recv_sem):
        pltpu.make_async_remote_copy(
            src_ref=dst,
            dst_ref=dst,
            send_sem=recv_sem,
            recv_sem=recv_sem,
            device_id=device(dc=1),
            device_id_type=MESH,
        ).wait_recv()

    def half(column, h):
        return uj.at[column, pl.ds(h * HALF, HALF)]

    def x_spread(cond, h):
        for column, dx in ((3, 2), (1, 1), (2, 3)):
            send(
                cond,
                half(0, h),
                half(column, h),
                x_send.at[column - 1, h],
                x_recv.at[column - 1, h],
                device(dx=dx),
            )

    for h, k in enumerate(steps):
        at = pl.ds(pl.multiple_of(own_at + h * HALF, HALF), HALF)
        send(k != 0, ui.at[at], half(0, h), z_send.at[h], z_recv.at[h], device(to_z=z_to[h]))
    for h, k in enumerate(steps):
        x_spread(k == 0, h)
    rows_of = ui.at[own_rows]
    send(None, rows_of, rows_of, row_send.at[0], row_recv.at[0], device(dc=1))
    send(None, rows_of, rows_of, row_send.at[1], row_recv.at[1], device(to_z=z_pair))

    def take_half(cond, h):
        @pl.when(cond)
        def _():
            arrived(half(0, h), z_recv.at[h])

        x_spread(cond, h)

    take_half(jnp.logical_or(y == 1, y == 3), 0)
    take_half(jnp.logical_or(y == 0, y == 2), 1)
    take_half(y == 2, 0)
    take_half(y == 1, 1)
    arrived(ui.at[pair_rows], row_recv.at[1])
    rows_of = ui.at[pair_rows]
    send(None, rows_of, rows_of, row_send.at[2], row_recv.at[2], device(dc=1))
    arrived(ui.at[sib_rows], row_recv.at[0])
    arrived(ui.at[last_rows], row_recv.at[2])

    def scores(column):
        high, low = split(uj[column])
        uj_hi[column] = high
        uj_lo[column] = low
        for part in range(2):
            rows = slice(part * 2 * ROWS, (part + 1) * 2 * ROWS)
            left, left_low = ui_hi[rows, :], ui_lo[rows, :]
            score = dot_nt(left, high) + dot_nt(left_low, high) + dot_nt(left, low)
            weight = jnp.exp(score * INV_TEMP - INV_TEMP)
            if column == 0:
                col = lax.broadcasted_iota(jnp.int32, (1, ROWS), 1)
                first = jnp.where(y == 0, 0, HALF)
                kept = jnp.logical_or(y == 0, y == YS - 1)
                start = jnp.where(kept, own_at - part * 2 * ROWS, 4 * ALL)
                inside = jnp.logical_and(col >= first, col < first + HALF)
                diagonal = jnp.where(inside, col + start, 4 * ALL)
                row = lax.broadcasted_iota(jnp.int32, weight.shape, 0)
                weight = jnp.where(row == diagonal, 0.0, weight)
                acc[rows, :] = weight
            else:
                acc[rows, :] += weight
            weights[column, rows, :] = weight

    high, low = split(ui[...])
    ui_hi[...] = high
    ui_lo[...] = low
    for column in range(XS):
        if column:
            for h in range(2):
                arrived(half(column, h), x_recv.at[column - 1, h])
        scores(column)

    mine = (y * 2 + odd) * CORES + core
    ones = jnp.ones((8, ROWS), F32)
    for i in range(8):
        part = acc[i * HALF : (i + 1) * HALF, :]
        sums[mine, i] = dot_nt(ones, part, HIGHEST)[0:1]
    for i, (dy, db, dc) in enumerate(group):
        send(
            None,
            sums.at[mine],
            sums.at[mine],
            sums_send.at[i],
            sums_recv.at[mine],
            device(dy=dy, to_z=z_pair if db else z, dc=dc),
        )
    partner_copy.wait()
    unit = ui[own_rows, :]
    node = lax.broadcasted_iota(jnp.int32, (ROWS, ROWS), 0)
    pairing = (node + blk * ROWS == partner_ref[...]).astype(F32)
    mate = dot_nn(pairing, unit, HIGHEST)
    mates[...] = mate
    pair_score = dot_nt(jnp.ones((8, WIDTH), F32), unit * mate, HIGHEST)[0:1]
    for dy, db, dc in group:
        other_b = 1 - odd if db else odd
        other = (lax.rem(y + dy, YS) * 2 + other_b) * CORES + lax.rem(core + dc, CORES)
        arrived(sums.at[other], sums_recv.at[other])
    total = sums[0]
    for i in range(1, 4 * YS):
        total = total + sums[i]
    inverse[...] = 1.0 / total

    for h, k in enumerate(steps):
        for column, dx in ((3, 2), (1, 1), (2, 3), (0, 0)):
            send(
                k != 0 if column == 0 else None,
                inverse.at[(core * 2 + odd) * 2 + h],
                inverse_cols.at[column, h],
                inv_send.at[column, h],
                inv_recv.at[column, h],
                device(dx=dx, to_z=z_to[h]),
            )

        @pl.when(k == 0)
        def _():
            inverse_cols[0, h] = inverse[(core * 2 + odd) * 2 + h]

    own_inverse = jnp.concatenate(
        [inverse[(core * 2 + odd) * 2], inverse[(core * 2 + odd) * 2 + 1]], axis=1
    )
    loss_ref[...] = INV_TEMP - jnp.log(own_inverse) - INV_TEMP * pair_score
    same = lax.broadcasted_iota(jnp.int32, (ROWS, ROWS), 1) == node
    for i in range(4):
        row = jnp.concatenate([inverse[2 * i], inverse[2 * i + 1]], axis=1)
        column_sum = jnp.sum(jnp.where(same, row, 0.0), axis=1, keepdims=True)
        inverse_rows[i * ROWS : (i + 1) * ROWS, :] = jnp.broadcast_to(column_sum, (ROWS, ROWS))
    for column in range(XS):
        for h, k in enumerate(steps):
            if column:
                arrived(inverse_cols.at[column, h], inv_recv.at[column, h])
            else:

                @pl.when(k != 0)
                def _():
                    arrived(inverse_cols.at[column, h], inv_recv.at[column, h])

    def pulls(first):
        rows = pl.ds(pl.multiple_of(first, 2 * ROWS), 2 * ROWS)
        total = jnp.zeros((2 * ROWS, WIDTH), F32)
        for column in range(XS):
            across = jnp.concatenate([inverse_cols[column, 0], inverse_cols[column, 1]], axis=1)
            both = weights[column, rows, :] * (inverse_rows[rows, :] + across)
            high, low = split(both)
            total = total + dot_nn(high, uj_hi[column])
            total = total + dot_nn(low, uj_hi[column])
            total = total + dot_nn(high, uj_lo[column])
        return total

    pull_out[...] = pulls((1 - core) * 2 * ROWS)
    send(None, pull_out, pull_in, sib_send, sib_recv, device(dc=1))
    pull_own[...] = pulls(core * 2 * ROWS)
    arrived(pull_in, sib_recv)
    pull_own[...] += pull_in[...]

    def share(block, at):
        return pl.ds(pl.multiple_of(block * ROWS + at * SHARE, SHARE), SHARE)

    for db in (1, 0):
        for dy in range(1 - db, YS):
            slot = dy + 3 if db else dy - 1
            send(
                None,
                pull_own.at[share(1 - odd if db else odd, lax.rem(y + dy, YS))],
                shares.at[slot],
                share_send.at[slot],
                share_recv.at[slot],
                device(dy=dy, to_z=z_pair if db else z),
            )
    for slot in range(7):
        arrived(shares.at[slot], share_recv.at[slot])
    rows = pl.ds(pl.multiple_of(y * SHARE, SHARE), SHARE)
    pull = pull_own[share(odd, y), :]
    for slot in range(7):
        pull = pull + shares[slot]
    unit = ui[pl.ds(pl.multiple_of(own_at + y * SHARE, SHARE), SHARE), :]
    grad_unit = INV_TEMP * (pull - 2.0 * mates[rows, :])
    along = jnp.sum(unit * grad_unit, axis=1, keepdims=True)
    grad_ref[rows, :] = (grad_unit - unit * along) / norms[rows, :]
    for dy in range(1, YS):
        send(
            None,
            grad_ref.at[rows],
            grad_ref.at[rows],
            grad_send.at[dy - 1],
            grad_recv.at[dy - 1],
            device(dy=dy),
        )
    for dy in range(1, YS):
        from_rows = pl.ds(pl.multiple_of(lax.rem(y + YS - dy, YS) * SHARE, SHARE), SHARE)
        arrived(grad_ref.at[from_rows], grad_recv.at[dy - 1])
    for cond, copy in sent:
        if cond is None:
            copy.wait_send()
        else:
            pl.when(cond)(copy.wait_send)


def body(embeddings, partner):
    vmem = pl.BlockSpec(memory_space=pltpu.VMEM)
    hbm = pl.BlockSpec(memory_space=pl.ANY)
    dma = pltpu.SemaphoreType.DMA
    loss, grad = pl.pallas_call(
        kernel,
        out_shape=(
            jax.ShapeDtypeStruct((1, ROWS), F32),
            jax.ShapeDtypeStruct((ROWS, WIDTH), F32),
        ),
        in_specs=[hbm, hbm],
        out_specs=(vmem, vmem),
        scratch_shapes=[
            pltpu.VMEM((ROWS, WIDTH), F32),
            pltpu.VMEM((1, ROWS), jnp.int32),
            pltpu.VMEM((ALL, WIDTH), F32),
            pltpu.VMEM((ALL, WIDTH), BF16),
            pltpu.VMEM((ALL, WIDTH), BF16),
            pltpu.VMEM((ROWS, 1), F32),
            pltpu.VMEM((ROWS, WIDTH), F32),
            pltpu.VMEM((XS, ROWS, WIDTH), F32),
            pltpu.VMEM((XS, ROWS, WIDTH), BF16),
            pltpu.VMEM((XS, ROWS, WIDTH), BF16),
            pltpu.VMEM((XS, ALL, ROWS), F32),
            pltpu.VMEM((ALL, ROWS), F32),
            pltpu.VMEM((4 * YS, 8, 1, HALF), F32),
            pltpu.VMEM((8, 1, HALF), F32),
            pltpu.VMEM((ALL, ROWS), F32),
            pltpu.VMEM((XS, 2, 1, HALF), F32),
            pltpu.VMEM((2 * ROWS, WIDTH), F32),
            pltpu.VMEM((2 * ROWS, WIDTH), F32),
            pltpu.VMEM((2 * ROWS, WIDTH), F32),
            pltpu.VMEM((7, SHARE, WIDTH), F32),
            dma((2,)),
            dma((2,)),
            dma((2,)),
            dma((3, 2)),
            dma((3, 2)),
            dma((3,)),
            dma((3,)),
            dma((15,)),
            dma((16,)),
            dma((4, 2)),
            dma((4, 2)),
            dma,
            dma,
            dma((7,)),
            dma((7,)),
            dma((3,)),
            dma((3,)),
        ],
        compiler_params=pltpu.CompilerParams(
            collective_id=0, has_side_effects=True, vmem_limit_bytes=48 * 2**20
        ),
    )(embeddings, partner.reshape(1, ROWS))
    return loss.reshape(ROWS), grad


def solution(mesh):
    return jax.shard_map(
        body,
        mesh=mesh,
        in_specs=(P("blk", None), P("blk")),
        out_specs=(P("blk"), P("blk", None)),
        check_vma=False,
    )
```

time: 63.6 us -> 55.9 us (0.88)
  Pallas kernels: 59.9 us -> 52.3 us
    pallas_call x1, Pallas kernels: 59.9 us -> 52.3 us  [body(): pl.pallas_call(kernel, out_shape=(jax.ShapeDtypeStruct((1, ROWS), F32), j...]
where the time goes in v2:
time: 55.9 us; the launch traced here: 55.8 us
  Pallas kernels  52.3 us (94%)
  local copies, waits for them, and re-layouts  2.84 us (5%)
  between operations  0.65 us (1%)
    pallas_call x1, Pallas kernels, body(): pl.pallas_call(kernel, out_shape=(jax.ShapeDtypeStruct((1, ROWS), F32), j...  52.3 us
    unnamed x6, local copies, waits for them, and re-layouts  2.84 us

profile of v2, /device:TPU:1, one launch (start us, length us, event | category | flops | bytes accessed | tf_op | source)
XLA Modules:
  0.0 55.8 jit_solution(12297612759792853092)
XLA Ops:
  0.6 0.0 copy-start.1
  0.6 0.7 %copy-done.1 = s32[192]{0:T(256)S(1)} copy-done((s32[192]{0:T(256)S(1)}, s32[192]{0:T(256)}, u32[]{:S(2)}) %copy-start.1) | copy-done | bytes 792
  1.3 0.0 copy-start
  1.3 0.9 %copy-done = f32[192,256]{1,0:T(8,128)S(1)} copy-done((f32[192,256]{1,0:T(8,128)S(1)}, f32[192,256]{1,0:T(8,128)}, u32[]{:S(2)}) %copy-start) | copy-done | bytes 196632
  2.2 52.3 %shard_map.41 = (f32[1,192]{1,0:T(1,128)S(1)}, f32[192,256]{1,0:T(8,128)S(1)}) custom-call(f32[192,256]{1,0:T(8,128)S(1)} %copy-done, s32[1,192]{1,0:T(1,128)S(1)} %bitcast.2), custom_call_target="tpu_custom_call" | custom-call | tf_op jit(solution)/shard_map/pallas_call | solution.py:374
  54.6 0.6 %copy.6 = f32[192]{0:T(256)} copy(f32[192]{0:T(256)S(1)} %bitcast.3) | data formatting | bytes 1536
  55.1 0.7 %copy.7 = f32[192,256]{1,0:T(8,128)} copy(f32[192,256]{1,0:T(8,128)S(1)} %get-tuple-element.9) | data formatting | bytes 393216
Async XLA Ops:
  0.6 0.7 %copy-start.1 = (s32[192]{0:T(256)S(1)}, s32[192]{0:T(256)}, u32[]{:S(2)}) copy-start(s32[192]{0:T(256)} %param.3) | copy-start | bytes 2308
  1.3 0.9 %copy-start = (f32[192,256]{1,0:T(8,128)S(1)}, f32[192,256]{1,0:T(8,128)}, u32[]{:S(2)}) copy-start(f32[192,256]{1,0:T(8,128)} %emb_hbm.1) | copy-start | bytes 589828

commit v3 on v2

v3 whole, which is shorter than its diff:
```python
import functools

import jax
import jax.numpy as jnp
from jax import lax
from jax.experimental import pallas as pl
from jax.experimental.pallas import tpu as pltpu
from jax.sharding import PartitionSpec as P

MESH = pl.DeviceIdType.MESH
F32 = jnp.float32
BF16 = jnp.bfloat16
HIGHEST = lax.Precision.HIGHEST
INV_TEMP = 10.0
ROWS = 192
WIDTH = 256
XS, YS, ZS, CORES = 4, 4, 8, 2
QUARTER = ROWS // 4
SHARE = ROWS // YS
TILE = 128
PLACE = (0, 2, 1, 3)
ALL = 4 * ROWS


def dot_nn(a, b, precision=None):
    return lax.dot_general(
        a, b, (((1,), (0,)), ((), ())), precision=precision, preferred_element_type=F32
    )


def dot_nt(a, b, precision=None):
    return lax.dot_general(
        a, b, (((1,), (1,)), ((), ())), precision=precision, preferred_element_type=F32
    )


def split(value):
    high = value.astype(BF16)
    return high, (value - high.astype(F32)).astype(BF16)


def kernel(
    emb_hbm,
    partner_hbm,
    loss_ref,
    grad_ref,
    emb_ref,
    partner_ref,
    ui,
    ui_wide,
    norms,
    mates,
    uj,
    transit,
    uj_wide,
    uj_tall,
    weights,
    acc,
    sums,
    inverse,
    inverse_own,
    inverse_rows,
    inverse_cols,
    across,
    wide,
    pull_out,
    pull_in,
    pull_own,
    shares,
    local_sem,
    z_send,
    z_recv,
    x_send,
    x_recv,
    row_send,
    row_recv,
    sums_send,
    sums_recv,
    inv_send,
    inv_recv,
    sib_send,
    sib_recv,
    share_send,
    share_recv,
    grad_send,
    grad_recv,
):
    blk = lax.axis_index("blk")
    y = lax.axis_index("rep")
    core = lax.rem(blk, CORES)
    x = lax.rem(lax.div(blk, CORES), XS)
    z = lax.div(blk, CORES * XS)
    odd = lax.rem(z, 2)
    z_pair = z + 1 - 2 * odd

    def device(dx=0, dy=0, to_z=None, dc=0):
        there = (z if to_z is None else to_z) * XS + lax.rem(x + (dx % XS), XS)
        return (there * CORES + lax.rem(core + dc, CORES), lax.rem(y + (dy % YS), YS))

    quarters = [lax.rem(k + YS - y, 4) for k in range(4)]
    z_to = [
        lax.rem(z + ZS + jnp.where(lax.rem(z + k, 2) == 0, k, -k), ZS) for k in range(4)
    ]
    z_from = [lax.rem(z + ZS + jnp.where(odd == 0, -k, k), ZS) for k in range(4)]

    embedding_copy = pltpu.make_async_copy(emb_hbm, emb_ref, local_sem.at[0])
    partner_copy = pltpu.make_async_copy(partner_hbm, partner_ref, local_sem.at[1])
    embedding_copy.start()
    partner_copy.start()

    group = [
        (dy, db, dc)
        for dy in range(YS)
        for db in range(2)
        for dc in range(CORES)
        if (dy, db, dc) != (0, 0, 0)
    ]
    near = [device(dc=1), device(to_z=z_pair)]
    near += [device(dx=d) for d in (1, 2, 3)] + [device(dy=d) for d in (1, 2, 3)]
    near += [device(to_z=z_from[k]) for k in (1, 2, 3)]
    barrier = pltpu.get_barrier_semaphore()
    for peer in near:
        pl.semaphore_signal(barrier, inc=1, device_id=peer, device_id_type=MESH)
    own_at = (core * 2 + odd) * ROWS
    own_rows = pl.ds(pl.multiple_of(own_at, ROWS), ROWS)
    sib_rows = pl.ds(pl.multiple_of(((1 - core) * 2 + odd) * ROWS, ROWS), ROWS)
    pair_rows = pl.ds(pl.multiple_of((core * 2 + 1 - odd) * ROWS, ROWS), ROWS)
    last_rows = pl.ds(pl.multiple_of(((1 - core) * 2 + 1 - odd) * ROWS, ROWS), ROWS)

    embedding_copy.wait()
    emb = emb_ref[...]
    norm = jnp.sqrt(jnp.sum(emb * emb, axis=1, keepdims=True) + 1e-12)
    unit = emb / norm
    norms[...] = norm
    ui[own_rows, :] = unit
    first = pl.ds(pl.multiple_of(own_at + quarters[0] * QUARTER, QUARTER), QUARTER)
    uj[0:QUARTER, :] = ui[first, :]
    second = pl.ds(pl.multiple_of(own_at + quarters[1] * QUARTER, QUARTER), QUARTER)
    transit[0:QUARTER, :] = ui[second, :]

    pl.semaphore_wait(barrier, len(near))

    sent = []

    def send(src, dst, send_sem, recv_sem, peer):
        copy = pltpu.make_async_remote_copy(
            src_ref=src,
            dst_ref=dst,
            send_sem=send_sem,
            recv_sem=recv_sem,
            device_id=peer,
            device_id_type=MESH,
        )
        copy.start()
        sent.append(copy)

    def settle():
        for copy in sent:
            copy.wait_send()
        sent.clear()

    def arrived(dst, recv_sem):
        pltpu.make_async_remote_copy(
            src_ref=dst,
            dst_ref=dst,
            send_sem=recv_sem,
            recv_sem=recv_sem,
            device_id=device(dc=1),
            device_id_type=MESH,
        ).wait_recv()

    def quarter(k, column):
        return uj.at[pl.ds(PLACE[k] * ROWS + column * QUARTER, QUARTER)]

    def x_spread(k, place):
        for column, dx in ((3, 2), (1, 1), (2, 3)):
            send(
                place(0),
                place(column),
                x_send.at[k, column - 1],
                x_recv.at[k, column - 1],
                device(dx=dx),
            )

    def in_transit(column):
        return transit.at[pl.ds(column * QUARTER, QUARTER)]

    def x_arrived(k, place):
        for column in range(1, XS):
            arrived(place(column), x_recv.at[k, column - 1])

    for k in (3, 2):
        at = pl.ds(pl.multiple_of(own_at + quarters[k] * QUARTER, QUARTER), QUARTER)
        send(ui.at[at], quarter(k, 0), z_send.at[k - 1], z_recv.at[k - 1], device(to_z=z_to[k]))
    x_spread(1, in_transit)
    x_spread(0, functools.partial(quarter, 0))
    rows_of = ui.at[own_rows]
    send(rows_of, rows_of, row_send.at[0], row_recv.at[0], device(dc=1))
    send(rows_of, rows_of, row_send.at[1], row_recv.at[1], device(to_z=z_pair))
    arrived(quarter(2, 0), z_recv.at[1])
    x_spread(2, functools.partial(quarter, 2))
    x_arrived(1, in_transit)
    near_place = uj.at[pl.ds(PLACE[1] * ROWS, ROWS)]
    send(transit, near_place, z_send.at[0], z_recv.at[0], device(to_z=z_to[1]))
    arrived(quarter(3, 0), z_recv.at[2])
    x_spread(3, functools.partial(quarter, 3))
    arrived(ui.at[pair_rows], row_recv.at[1])
    rows_of = ui.at[pair_rows]
    send(rows_of, rows_of, row_send.at[2], row_recv.at[2], device(dc=1))
    arrived(ui.at[sib_rows], row_recv.at[0])
    arrived(ui.at[last_rows], row_recv.at[2])

    def scores(start, stop):
        high, low = split(uj[start:stop, :])
        for i, value in enumerate((high, high, low)):
            uj_wide[start:stop, i * WIDTH : (i + 1) * WIDTH] = value
            uj_tall[i * ALL + start : i * ALL + stop, :] = value
        score = dot_nt(ui_wide[...], uj_wide[start:stop, :])
        weight = jnp.exp(score * INV_TEMP - INV_TEMP)
        if start == 0:
            col = lax.broadcasted_iota(jnp.int32, (1, stop), 1)
            diagonal = jnp.where(col < QUARTER, col + own_at + quarters[0] * QUARTER, 4 * ALL)
            row = lax.broadcasted_iota(jnp.int32, weight.shape, 0)
            weight = jnp.where(row == diagonal, 0.0, weight)
        weights[:, start:stop] = weight
        tiles = [weight[:, i : i + TILE] for i in range(0, stop - start, TILE)]
        part = tiles[0]
        for tile in tiles[1:]:
            part = part + tile
        if start == 0:
            acc[...] = part
        else:
            acc[...] += part

    high, low = split(ui[...])
    for i, value in enumerate((high, low, high)):
        ui_wide[:, i * WIDTH : (i + 1) * WIDTH] = value
    x_arrived(0, functools.partial(quarter, 0))
    x_arrived(2, functools.partial(quarter, 2))
    scores(0, 384)
    arrived(near_place, z_recv.at[0])
    scores(384, 512)
    x_arrived(3, functools.partial(quarter, 3))
    scores(512, 768)

    gather_sent = list(sent)
    sent.clear()
    mine = (y * 2 + odd) * CORES + core
    ones = jnp.ones((8, TILE), BF16)
    for i in range(4):
        high, low = split(acc[i * ROWS : (i + 1) * ROWS, :])
        sums[mine, i] = (dot_nt(ones, high) + dot_nt(ones, low))[0:1]
    for i, (dy, db, dc) in enumerate(group):
        send(
            sums.at[mine],
            sums.at[mine],
            sums_send.at[i],
            sums_recv.at[mine],
            device(dy=dy, to_z=z_pair if db else z, dc=dc),
        )
    partner_copy.wait()
    unit = ui[own_rows, :]
    node = lax.broadcasted_iota(jnp.int32, (ROWS, ROWS), 0)
    pairing = (node + blk * ROWS == partner_ref[...]).astype(F32)
    mate = dot_nn(pairing, unit, HIGHEST)
    mates[...] = mate
    pair_score = dot_nt(jnp.ones((8, WIDTH), F32), unit * mate, HIGHEST)[0:1]
    sums_sent = list(sent)
    sent[:] = gather_sent
    settle()
    for dy, db, dc in group:
        other_b = 1 - odd if db else odd
        other = (lax.rem(y + dy, YS) * 2 + other_b) * CORES + lax.rem(core + dc, CORES)
        arrived(sums.at[other], sums_recv.at[other])
    total = sums[0]
    for i in range(1, 4 * YS):
        total = total + sums[i]
    inverse[...] = 1.0 / total

    own_inverse = inverse[core * 2 + odd]
    for i in range(4):
        inverse_own[i] = own_inverse[:, i * QUARTER : (i + 1) * QUARTER]

    for k in (3, 2, 1, 0):
        for column, dx in ((3, 2), (1, 1), (2, 3), (0, 0)):
            if (k, column) != (0, 0):
                send(
                    inverse_own.at[quarters[k]],
                    inverse_cols.at[k, column],
                    inv_send.at[k, column],
                    inv_recv.at[k, column],
                    device(dx=dx, to_z=z_to[k]),
                )
    inverse_cols[0, 0] = inverse_own[quarters[0]]
    loss_ref[...] = INV_TEMP - jnp.log(own_inverse) - INV_TEMP * pair_score
    same = lax.broadcasted_iota(jnp.int32, (ROWS, ROWS), 1) == node
    for i in range(4):
        column_sum = jnp.sum(jnp.where(same, inverse[i], 0.0), axis=1, keepdims=True)
        inverse_rows[i * ROWS : (i + 1) * ROWS, :] = jnp.broadcast_to(column_sum, (ROWS, TILE))
    inverse_sent = list(sent)
    sent[:] = sums_sent
    settle()
    for k in range(4):
        for column in range(XS):
            if (k, column) != (0, 0):
                arrived(inverse_cols.at[k, column], inv_recv.at[k, column])
    across[...] = jnp.concatenate(
        [inverse_cols[k, column] for k in PLACE for column in range(XS)], axis=1
    )

    def pulls(part, block):
        rows = pl.ds(pl.multiple_of(block * ROWS, ROWS), ROWS)
        for start in range(0, ALL, TILE):
            tile = slice(start, start + TILE)
            both = weights[rows, tile] * (inverse_rows[rows, :] + across[:, tile])
            high, low = split(both)
            for i, value in enumerate((high, low, high)):
                wide[part, :, i * ALL + start : i * ALL + start + TILE] = value
        return dot_nn(wide[part], uj_tall[...])

    there = (1 - odd, odd)
    for i in range(2):
        pull_out[i] = pulls(i, (1 - core) * 2 + there[i])
        send(pull_out.at[i], pull_in.at[i], sib_send.at[i], sib_recv.at[i], device(dc=1))
    for i in range(2):
        pull_own[i] = pulls(2 + i, core * 2 + there[i])

    def share(at):
        return pl.ds(pl.multiple_of(at * SHARE, SHARE), SHARE)

    for i in range(2):
        arrived(pull_in.at[i], sib_recv.at[i])
        pull_own[i] += pull_in[i]
        for dy in range(i, YS):
            slot = dy - 1 if i else dy + 3
            send(
                pull_own.at[i, share(lax.rem(y + dy, YS))],
                shares.at[slot],
                share_send.at[slot],
                share_recv.at[slot],
                device(dy=dy, to_z=z if i else z_pair),
            )
    shares_sent = list(sent)
    sent[:] = inverse_sent
    settle()
    for slot in range(7):
        arrived(shares.at[slot], share_recv.at[slot])
    rows = pl.ds(pl.multiple_of(y * SHARE, SHARE), SHARE)
    pull = pull_own[1, share(y), :]
    for slot in range(7):
        pull = pull + shares[slot]
    unit = ui[pl.ds(pl.multiple_of(own_at + y * SHARE, SHARE), SHARE), :]
    grad_unit = INV_TEMP * (pull - 2.0 * mates[rows, :])
    along = jnp.sum(unit * grad_unit, axis=1, keepdims=True)
    grad_ref[rows, :] = (grad_unit - unit * along) / norms[rows, :]
    for dy in range(1, YS):
        send(
            grad_ref.at[rows],
            grad_ref.at[rows],
            grad_send.at[dy - 1],
            grad_recv.at[dy - 1],
            device(dy=dy),
        )
    sent.extend(shares_sent)
    settle()
    for dy in range(1, YS):
        from_rows = pl.ds(pl.multiple_of(lax.rem(y + YS - dy, YS) * SHARE, SHARE), SHARE)
        arrived(grad_ref.at[from_rows], grad_recv.at[dy - 1])
    settle()


def body(embeddings, partner):
    vmem = pl.BlockSpec(memory_space=pltpu.VMEM)
    hbm = pl.BlockSpec(memory_space=pltpu.HBM)
    dma = pltpu.SemaphoreType.DMA
    loss, grad = pl.pallas_call(
        kernel,
        out_shape=(
            jax.ShapeDtypeStruct((1, ROWS), F32),
            jax.ShapeDtypeStruct((ROWS, WIDTH), F32),
        ),
        in_specs=[hbm, hbm],
        out_specs=(vmem, vmem),
        scratch_shapes=[
            pltpu.VMEM((ROWS, WIDTH), F32),
            pltpu.VMEM((1, ROWS), jnp.int32),
            pltpu.VMEM((ALL, WIDTH), F32),
            pltpu.VMEM((ALL, 3 * WIDTH), BF16),
            pltpu.VMEM((ROWS, 1), F32),
            pltpu.VMEM((ROWS, WIDTH), F32),
            pltpu.VMEM((ALL, WIDTH), F32),
            pltpu.VMEM((ROWS, WIDTH), F32),
            pltpu.VMEM((ALL, 3 * WIDTH), BF16),
            pltpu.VMEM((3 * ALL, WIDTH), BF16),
            pltpu.VMEM((ALL, ALL), F32),
            pltpu.VMEM((ALL, TILE), F32),
            pltpu.VMEM((4 * YS, 4, 1, ROWS), F32),
            pltpu.VMEM((4, 1, ROWS), F32),
            pltpu.VMEM((4, 1, QUARTER), F32),
            pltpu.VMEM((ALL, TILE), F32),
            pltpu.VMEM((4, XS, 1, QUARTER), F32),
            pltpu.VMEM((1, ALL), F32),
            pltpu.VMEM((4, ROWS, 3 * ALL), BF16),
            pltpu.VMEM((2, ROWS, WIDTH), F32),
            pltpu.VMEM((2, ROWS, WIDTH), F32),
            pltpu.VMEM((2, ROWS, WIDTH), F32),
            pltpu.VMEM((7, SHARE, WIDTH), F32),
            dma((2,)),
            dma((3,)),
            dma((3,)),
            dma((4, 3)),
            dma((4, 3)),
            dma((3,)),
            dma((3,)),
            dma((15,)),
            dma((16,)),
            dma((4, 4)),
            dma((4, 4)),
            dma((2,)),
            dma((2,)),
            dma((7,)),
            dma((7,)),
            dma((3,)),
            dma((3,)),
        ],
        compiler_params=pltpu.CompilerParams(
            collective_id=0, has_side_effects=True, vmem_limit_bytes=56254464
        ),
    )(embeddings, partner.reshape(1, ROWS))
    return loss.reshape(ROWS), grad


def solution(mesh):
    return jax.shard_map(
        body,
        mesh=mesh,
        in_specs=(P("blk", None), P("blk")),
        out_specs=(P("blk"), P("blk", None)),
        check_vma=False,
    )
```

time: 55.9 us -> 49.2 us (0.88)
  Pallas kernels: 52.3 us -> 46.5 us
  local copies, waits for them, and re-layouts: 2.84 us -> 1.91 us
    pallas_call x1, Pallas kernels: 52.3 us -> 46.5 us  [body(): pl.pallas_call(kernel, out_shape=(jax.ShapeDtypeStruct((1, ROWS), F32), j...]
    unnamed x6 -> x4, local copies, waits for them, and re-layouts: 2.84 us -> 1.91 us
where the time goes in v3:
time: 49.2 us; the launch traced here: 49.1 us
  Pallas kernels  46.5 us (95%)
  local copies, waits for them, and re-layouts  1.91 us (4%)
  between operations  0.65 us (1%)
    pallas_call x1, Pallas kernels, body(): pl.pallas_call(kernel, out_shape=(jax.ShapeDtypeStruct((1, ROWS), F32), j...  46.5 us
    unnamed x4, local copies, waits for them, and re-layouts  1.91 us

profile of v3, /device:TPU:1, one launch (start us, length us, event | category | flops | bytes accessed | tf_op | source)
XLA Modules:
  0.0 49.1 jit_solution(7289868606056318820)
XLA Ops:
  0.6 0.0 copy-start
  0.6 0.7 %copy-done = s32[192]{0:T(256)S(1)} copy-done((s32[192]{0:T(256)S(1)}, s32[192]{0:T(256)}, u32[]{:S(2)}) %copy-start) | copy-done | bytes 792
  1.3 46.5 %shard_map.41 = (f32[1,192]{1,0:T(1,128)S(1)}, f32[192,256]{1,0:T(8,128)S(1)}) custom-call(f32[192,256]{1,0:T(8,128)} %emb_hbm.1, s32[1,192]{1,0:T(1,128)S(1)} %bitcast.2), custom_call_target="tpu_custom_call" | custom-call | tf_op jit(solution)/shard_map/pallas_call | solution.py:376
  47.8 0.6 %copy.6 = f32[192]{0:T(256)} copy(f32[192]{0:T(256)S(1)} %bitcast.3) | data formatting | bytes 1536
  48.4 0.7 %copy.7 = f32[192,256]{1,0:T(8,128)} copy(f32[192,256]{1,0:T(8,128)S(1)} %get-tuple-element.9) | data formatting | bytes 393216
Async XLA Ops:
  0.6 0.7 %copy-start = (s32[192]{0:T(256)S(1)}, s32[192]{0:T(256)}, u32[]{:S(2)}) copy-start(s32[192]{0:T(256)} %param.3) | copy-start | bytes 2308

commit v4 on v3

--- a/solution.py
+++ b/solution.py
@@ -1,4 +1,4 @@
-import functools
+import math
 
 import jax
 import jax.numpy as jnp
@@ -12,13 +12,13 @@
 BF16 = jnp.bfloat16
 HIGHEST = lax.Precision.HIGHEST
 INV_TEMP = 10.0
+EXP_SCALE = INV_TEMP * math.log2(math.e)
 ROWS = 192
 WIDTH = 256
 XS, YS, ZS, CORES = 4, 4, 8, 2
 QUARTER = ROWS // 4
 SHARE = ROWS // YS
 TILE = 128
-PLACE = (0, 2, 1, 3)
 ALL = 4 * ROWS
 
 
@@ -50,8 +50,8 @@
     ui_wide,
     norms,
     mates,
+    pair_scores,
     uj,
-    transit,
     uj_wide,
     uj_tall,
     weights,
@@ -63,13 +63,12 @@
     inverse_cols,
     across,
     wide,
+    pull_first,
     pull_out,
     pull_in,
     pull_own,
     shares,
     local_sem,
-    z_send,
-    z_recv,
     x_send,
     x_recv,
     row_send,
@@ -115,9 +114,11 @@
         for dc in range(CORES)
         if (dy, db, dc) != (0, 0, 0)
     ]
+    group.sort(key=lambda to: -(min(to[0], YS - to[0]) + to[1]))
     near = [device(dc=1), device(to_z=z_pair)]
     near += [device(dx=d) for d in (1, 2, 3)] + [device(dy=d) for d in (1, 2, 3)]
     near += [device(to_z=z_from[k]) for k in (1, 2, 3)]
+    near += [device(dx=d, to_z=z_from[1]) for d in (1, 2, 3)]
     barrier = pltpu.get_barrier_semaphore()
     for peer in near:
         pl.semaphore_signal(barrier, inc=1, device_id=peer, device_id_type=MESH)
@@ -135,9 +136,6 @@
     ui[own_rows, :] = unit
     first = pl.ds(pl.multiple_of(own_at + quarters[0] * QUARTER, QUARTER), QUARTER)
     uj[0:QUARTER, :] = ui[first, :]
-    second = pl.ds(pl.multiple_of(own_at + quarters[1] * QUARTER, QUARTER), QUARTER)
-    transit[0:QUARTER, :] = ui[second, :]
-
     pl.semaphore_wait(barrier, len(near))
 
     sent = []
@@ -170,40 +168,48 @@
         ).wait_recv()
 
     def quarter(k, column):
-        return uj.at[pl.ds(PLACE[k] * ROWS + column * QUARTER, QUARTER)]
-
-    def x_spread(k, place):
-        for column, dx in ((3, 2), (1, 1), (2, 3)):
+        return uj.at[pl.ds(k * ROWS + column * QUARTER, QUARTER)]
+
+    around = ((3, 2), (1, 1), (2, 3))
+
+    def x_spread(k):
+        for column, dx in around:
             send(
-                place(0),
-                place(column),
-                x_send.at[k, column - 1],
-                x_recv.at[k, column - 1],
+                quarter(k, 0),
+                quarter(k, column),
+                x_send.at[k, column],
+                x_recv.at[k, column],
                 device(dx=dx),
             )
 
-    def in_transit(column):
-        return transit.at[pl.ds(column * QUARTER, QUARTER)]
-
-    def x_arrived(k, place):
-        for column in range(1, XS):
-            arrived(place(column), x_recv.at[k, column - 1])
+    def own_quarter(k):
+        at = own_at + quarters[k] * QUARTER
+        return ui.at[pl.ds(pl.multiple_of(at, QUARTER), QUARTER)]
 
     for k in (3, 2):
-        at = pl.ds(pl.multiple_of(own_at + quarters[k] * QUARTER, QUARTER), QUARTER)
-        send(ui.at[at], quarter(k, 0), z_send.at[k - 1], z_recv.at[k - 1], device(to_z=z_to[k]))
-    x_spread(1, in_transit)
-    x_spread(0, functools.partial(quarter, 0))
+        send(own_quarter(k), quarter(k, 0), x_send.at[k, 0], x_recv.at[k, 0], device(to_z=z_to[k]))
+    for column, dx in around + ((0, 0),):
+        send(
+            own_quarter(1),
+            quarter(1, column),
+            x_send.at[1, column],
+            x_recv.at[1, column],
+            device(dx=dx, to_z=z_to[1]),
+        )
+    x_spread(0)
     rows_of = ui.at[own_rows]
     send(rows_of, rows_of, row_send.at[0], row_recv.at[0], device(dc=1))
     send(rows_of, rows_of, row_send.at[1], row_recv.at[1], device(to_z=z_pair))
-    arrived(quarter(2, 0), z_recv.at[1])
-    x_spread(2, functools.partial(quarter, 2))
-    x_arrived(1, in_transit)
-    near_place = uj.at[pl.ds(PLACE[1] * ROWS, ROWS)]
-    send(transit, near_place, z_send.at[0], z_recv.at[0], device(to_z=z_to[1]))
-    arrived(quarter(3, 0), z_recv.at[2])
-    x_spread(3, functools.partial(quarter, 3))
+    partner_copy.wait()
+    unit = ui[own_rows, :]
+    node = lax.broadcasted_iota(jnp.int32, (ROWS, ROWS), 0)
+    pairing = (node + blk * ROWS == partner_ref[...]).astype(F32)
+    mate = dot_nn(pairing, unit, HIGHEST)
+    mates[...] = mate
+    pair_scores[...] = dot_nt(jnp.ones((8, WIDTH), F32), unit * mate, HIGHEST)[0:1]
+    for k in (2, 3):
+        arrived(quarter(k, 0), x_recv.at[k, 0])
+        x_spread(k)
     arrived(ui.at[pair_rows], row_recv.at[1])
     rows_of = ui.at[pair_rows]
     send(rows_of, rows_of, row_send.at[2], row_recv.at[2], device(dc=1))
@@ -214,9 +220,11 @@
         high, low = split(uj[start:stop, :])
         for i, value in enumerate((high, high, low)):
             uj_wide[start:stop, i * WIDTH : (i + 1) * WIDTH] = value
-            uj_tall[i * ALL + start : i * ALL + stop, :] = value
+            half = ALL // 2
+            at = i * half + start % half
+            uj_tall[start // half, at : at + stop - start, :] = value
         score = dot_nt(ui_wide[...], uj_wide[start:stop, :])
-        weight = jnp.exp(score * INV_TEMP - INV_TEMP)
+        weight = jnp.exp2(score * EXP_SCALE - EXP_SCALE)
         if start == 0:
             col = lax.broadcasted_iota(jnp.int32, (1, stop), 1)
             diagonal = jnp.where(col < QUARTER, col + own_at + quarters[0] * QUARTER, 4 * ALL)
@@ -235,12 +243,16 @@
     high, low = split(ui[...])
     for i, value in enumerate((high, low, high)):
         ui_wide[:, i * WIDTH : (i + 1) * WIDTH] = value
-    x_arrived(0, functools.partial(quarter, 0))
-    x_arrived(2, functools.partial(quarter, 2))
+    def await_columns(k, start):
+        for column in range(start, XS):
+            arrived(quarter(k, column), x_recv.at[k, column])
+
+    await_columns(0, 1)
+    await_columns(1, 0)
     scores(0, 384)
-    arrived(near_place, z_recv.at[0])
+    await_columns(2, 1)
     scores(384, 512)
-    x_arrived(3, functools.partial(quarter, 3))
+    await_columns(3, 1)
     scores(512, 768)
 
     gather_sent = list(sent)
@@ -258,13 +270,6 @@
             sums_recv.at[mine],
             device(dy=dy, to_z=z_pair if db else z, dc=dc),
         )
-    partner_copy.wait()
-    unit = ui[own_rows, :]
-    node = lax.broadcasted_iota(jnp.int32, (ROWS, ROWS), 0)
-    pairing = (node + blk * ROWS == partner_ref[...]).astype(F32)
-    mate = dot_nn(pairing, unit, HIGHEST)
-    mates[...] = mate
-    pair_score = dot_nt(jnp.ones((8, WIDTH), F32), unit * mate, HIGHEST)[0:1]
     sums_sent = list(sent)
     sent[:] = gather_sent
     settle()
@@ -292,7 +297,7 @@
                     device(dx=dx, to_z=z_to[k]),
                 )
     inverse_cols[0, 0] = inverse_own[quarters[0]]
-    loss_ref[...] = INV_TEMP - jnp.log(own_inverse) - INV_TEMP * pair_score
+    loss_ref[...] = INV_TEMP - jnp.log(own_inverse) - INV_TEMP * pair_scores[...]
     same = lax.broadcasted_iota(jnp.int32, (ROWS, ROWS), 1) == node
     for i in range(4):
         column_sum = jnp.sum(jnp.where(same, inverse[i], 0.0), axis=1, keepdims=True)
@@ -300,30 +305,39 @@
     inverse_sent = list(sent)
     sent[:] = sums_sent
     settle()
-    for k in range(4):
-        for column in range(XS):
-            if (k, column) != (0, 0):
-                arrived(inverse_cols.at[k, column], inv_recv.at[k, column])
-    across[...] = jnp.concatenate(
-        [inverse_cols[k, column] for k in PLACE for column in range(XS)], axis=1
-    )
-
-    def pulls(part, block):
+    def take_inverse(part):
+        columns = slice(part * ALL // 2, (part + 1) * ALL // 2)
+        pieces = []
+        for k in (2 * part, 2 * part + 1):
+            for column in range(XS):
+                if (k, column) != (0, 0):
+                    arrived(inverse_cols.at[k, column], inv_recv.at[k, column])
+                pieces.append((k, column))
+        across[:, columns] = jnp.concatenate([inverse_cols[piece] for piece in pieces], axis=1)
+
+    def pulls(slot, block, part):
         rows = pl.ds(pl.multiple_of(block * ROWS, ROWS), ROWS)
-        for start in range(0, ALL, TILE):
-            tile = slice(start, start + TILE)
+        size = ALL // 2
+        for start in range(0, size, TILE):
+            tile = slice(part * size + start, part * size + start + TILE)
             both = weights[rows, tile] * (inverse_rows[rows, :] + across[:, tile])
             high, low = split(both)
             for i, value in enumerate((high, low, high)):
-                wide[part, :, i * ALL + start : i * ALL + start + TILE] = value
-        return dot_nn(wide[part], uj_tall[...])
+                wide[slot, :, i * size + start : i * size + start + TILE] = value
+        return dot_nn(wide[slot], uj_tall[part])
 
     there = (1 - odd, odd)
+    blocks = [(1 - core) * 2 + b for b in there] + [core * 2 + b for b in there]
+    take_inverse(0)
+    for i, block in enumerate(blocks):
+        pull_first[i] = pulls(i, block, 0)
+    take_inverse(1)
+
     for i in range(2):
-        pull_out[i] = pulls(i, (1 - core) * 2 + there[i])
+        pull_out[i] = pull_first[i] + pulls(i, blocks[i], 1)
         send(pull_out.at[i], pull_in.at[i], sib_send.at[i], sib_recv.at[i], device(dc=1))
     for i in range(2):
-        pull_own[i] = pulls(2 + i, core * 2 + there[i])
+        pull_own[i] = pull_first[2 + i] + pulls(2 + i, blocks[2 + i], 1)
 
     def share(at):
         return pl.ds(pl.multiple_of(at * SHARE, SHARE), SHARE)
@@ -331,7 +345,7 @@
     for i in range(2):
         arrived(pull_in.at[i], sib_recv.at[i])
         pull_own[i] += pull_in[i]
-        for dy in range(i, YS):
+        for dy in (2, 1, 3) if i else (2, 1, 3, 0):
             slot = dy - 1 if i else dy + 3
             send(
                 pull_own.at[i, share(lax.rem(y + dy, YS))],
@@ -353,7 +367,7 @@
     grad_unit = INV_TEMP * (pull - 2.0 * mates[rows, :])
     along = jnp.sum(unit * grad_unit, axis=1, keepdims=True)
     grad_ref[rows, :] = (grad_unit - unit * along) / norms[rows, :]
-    for dy in range(1, YS):
+    for dy in (2, 1, 3):
         send(
             grad_ref.at[rows],
             grad_ref.at[rows],
@@ -388,10 +402,10 @@
             pltpu.VMEM((ALL, 3 * WIDTH), BF16),
             pltpu.VMEM((ROWS, 1), F32),
             pltpu.VMEM((ROWS, WIDTH), F32),
+            pltpu.VMEM((1, ROWS), F32),
             pltpu.VMEM((ALL, WIDTH), F32),
-            pltpu.VMEM((ROWS, WIDTH), F32),
             pltpu.VMEM((ALL, 3 * WIDTH), BF16),
-            pltpu.VMEM((3 * ALL, WIDTH), BF16),
+            pltpu.VMEM((2, 3 * ALL // 2, WIDTH), BF16),
             pltpu.VMEM((ALL, ALL), F32),
             pltpu.VMEM((ALL, TILE), F32),
             pltpu.VMEM((4 * YS, 4, 1, ROWS), F32),
@@ -400,16 +414,15 @@
             pltpu.VMEM((ALL, TILE), F32),
             pltpu.VMEM((4, XS, 1, QUARTER), F32),
             pltpu.VMEM((1, ALL), F32),
-            pltpu.VMEM((4, ROWS, 3 * ALL), BF16),
+            pltpu.VMEM((4, ROWS, 3 * ALL // 2), BF16),
+            pltpu.VMEM((4, ROWS, WIDTH), F32),
             pltpu.VMEM((2, ROWS, WIDTH), F32),
             pltpu.VMEM((2, ROWS, WIDTH), F32),
             pltpu.VMEM((2, ROWS, WIDTH), F32),
             pltpu.VMEM((7, SHARE, WIDTH), F32),
             dma((2,)),
-            dma((3,)),
-            dma((3,)),
-            dma((4, 3)),
-            dma((4, 3)),
+            dma((4, 4)),
+            dma((4, 4)),
             dma((3,)),
             dma((3,)),
             dma((15,)),
@@ -427,6 +440,27 @@
             collective_id=0, has_side_effects=True, vmem_limit_bytes=56254464
         ),
     )(embeddings, partner.reshape(1, ROWS))
+    def write(loss_vmem, grad_vmem, loss_out, grad_out, sems):
+        copies = [
+            pltpu.make_async_copy(grad_vmem, grad_out, sems.at[0]),
+            pltpu.make_async_copy(loss_vmem, loss_out, sems.at[1]),
+        ]
+        for copy in copies:
+            copy.start()
+        for copy in copies:
+            copy.wait()
+
+    loss, grad = pl.pallas_call(
+        write,
+        out_shape=(
+            jax.ShapeDtypeStruct((1, ROWS), F32),
+            jax.ShapeDtypeStruct((ROWS, WIDTH), F32),
+        ),
+        in_specs=[pl.BlockSpec(memory_space=pl.ANY)] * 2,
+        out_specs=(hbm, hbm),
+        scratch_shapes=[dma((2,))],
+        compiler_params=pltpu.CompilerParams(vmem_limit_bytes=2**20),
+    )(loss, grad)
     return loss.reshape(ROWS), grad
 
 

time: 49.2 us -> 47.8 us (0.972)
  local copies, waits for them, and re-layouts: 1.91 us -> 0.67 us
    unnamed x4 -> x2, local copies, waits for them, and re-layouts: 1.91 us -> 0.67 us
    pallas_call x1, Pallas kernels: 46.5 us -> 45.7 us  [body(): pl.pallas_call(kernel, out_shape=(jax.ShapeDtypeStruct((1, ROWS), F32), j...]
    pallas_call x0 -> x1, Pallas kernels: none -> 0.7 us  [body(): pl.pallas_call(write, out_shape=(jax.ShapeDtypeStruct((1, ROWS), F32), ja...]
where the time goes in v4:
time: 47.8 us; the launch traced here: 47.7 us
  Pallas kernels  46.4 us (97%)
  local copies, waits for them, and re-layouts  0.67 us (1%)
  between operations  0.65 us (1%)
    pallas_call x1, Pallas kernels, body(): pl.pallas_call(kernel, out_shape=(jax.ShapeDtypeStruct((1, ROWS), F32), j...  45.7 us

profile of v4, /device:TPU:1, one launch (start us, length us, event | category | flops | bytes accessed | tf_op | source)
XLA Modules:
  0.0 47.7 jit_solution(16750914297793067035)
XLA Ops:
  0.6 0.0 copy-start
  0.6 0.7 %copy-done = s32[192]{0:T(256)S(1)} copy-done((s32[192]{0:T(256)S(1)}, s32[192]{0:T(256)}, u32[]{:S(2)}) %copy-start) | copy-done | bytes 792
  1.3 45.7 %shard_map.41 = (f32[1,192]{1,0:T(1,128)S(1)}, f32[192,256]{1,0:T(8,128)S(1)}) custom-call(f32[192,256]{1,0:T(8,128)} %emb_hbm.1, s32[1,192]{1,0:T(1,128)S(1)} %bitcast.2), custom_call_target="tpu_custom_call" | custom-call | tf_op jit(solution)/shard_map/pallas_call | solution.py:390
  47.0 0.7 %shard_map.42 = (f32[1,192]{1,0:T(1,128)}, f32[192,256]{1,0:T(8,128)}) custom-call(f32[1,192]{1,0:T(1,128)S(1)} %get-tuple-element.6.loss_vmem, f32[192,256]{1,0:T(8,128)S(1)} %get-tuple-element.7.grad_vmem), custom_call_target="tpu_custom_call" | custom-call | tf_op jit(solution)/shard_map/pallas_call | solution.py:453
Async XLA Ops:
  0.6 0.7 %copy-start = (s32[192]{0:T(256)S(1)}, s32[192]{0:T(256)}, u32[]{:S(2)}) copy-start(s32[192]{0:T(256)} %param.3) | copy-start | bytes 2308

commit v5 on v4

--- a/solution.py
+++ b/solution.py
@@ -1,3 +1,4 @@
+import functools
 import math
 
 import jax
@@ -19,6 +20,7 @@
 QUARTER = ROWS // 4
 SHARE = ROWS // YS
 TILE = 128
+PLACE = (0, 2, 1, 3)
 ALL = 4 * ROWS
 
 
@@ -52,6 +54,7 @@
     mates,
     pair_scores,
     uj,
+    transit,
     uj_wide,
     uj_tall,
     weights,
@@ -69,6 +72,10 @@
     pull_own,
     shares,
     local_sem,
+    z_send,
+    z_recv,
+    near_send,
+    near_recv,
     x_send,
     x_recv,
     row_send,
@@ -118,15 +125,14 @@
     near = [device(dc=1), device(to_z=z_pair)]
     near += [device(dx=d) for d in (1, 2, 3)] + [device(dy=d) for d in (1, 2, 3)]
     near += [device(to_z=z_from[k]) for k in (1, 2, 3)]
-    near += [device(dx=d, to_z=z_from[1]) for d in (1, 2, 3)]
     barrier = pltpu.get_barrier_semaphore()
     for peer in near:
         pl.semaphore_signal(barrier, inc=1, device_id=peer, device_id_type=MESH)
-    own_at = (core * 2 + odd) * ROWS
+    own_at = (odd * 2 + core) * ROWS
     own_rows = pl.ds(pl.multiple_of(own_at, ROWS), ROWS)
-    sib_rows = pl.ds(pl.multiple_of(((1 - core) * 2 + odd) * ROWS, ROWS), ROWS)
-    pair_rows = pl.ds(pl.multiple_of((core * 2 + 1 - odd) * ROWS, ROWS), ROWS)
-    last_rows = pl.ds(pl.multiple_of(((1 - core) * 2 + 1 - odd) * ROWS, ROWS), ROWS)
+    sib_rows = pl.ds(pl.multiple_of((odd * 2 + 1 - core) * ROWS, ROWS), ROWS)
+    pair_rows = pl.ds(pl.multiple_of(((1 - odd) * 2 + core) * ROWS, ROWS), ROWS)
+    last_rows = pl.ds(pl.multiple_of(((1 - odd) * 2 + 1 - core) * ROWS, ROWS), ROWS)
 
     embedding_copy.wait()
     emb = emb_ref[...]
@@ -136,6 +142,9 @@
     ui[own_rows, :] = unit
     first = pl.ds(pl.multiple_of(own_at + quarters[0] * QUARTER, QUARTER), QUARTER)
     uj[0:QUARTER, :] = ui[first, :]
+    second = pl.ds(pl.multiple_of(own_at + quarters[1] * QUARTER, QUARTER), QUARTER)
+    transit[0:QUARTER, :] = ui[second, :]
+
     pl.semaphore_wait(barrier, len(near))
 
     sent = []
@@ -168,38 +177,46 @@
         ).wait_recv()
 
     def quarter(k, column):
-        return uj.at[pl.ds(k * ROWS + column * QUARTER, QUARTER)]
-
-    around = ((3, 2), (1, 1), (2, 3))
-
-    def x_spread(k):
-        for column, dx in around:
+        return uj.at[pl.ds(PLACE[k] * ROWS + column * QUARTER, QUARTER)]
+
+    def x_spread(k, place):
+        for column, dx in ((3, 2), (1, 1), (2, 3)):
             send(
-                quarter(k, 0),
-                quarter(k, column),
-                x_send.at[k, column],
-                x_recv.at[k, column],
+                place(0),
+                place(column),
+                x_send.at[k, column - 1],
+                x_recv.at[k, column - 1],
                 device(dx=dx),
             )
 
-    def own_quarter(k):
-        at = own_at + quarters[k] * QUARTER
-        return ui.at[pl.ds(pl.multiple_of(at, QUARTER), QUARTER)]
+    def in_transit(column):
+        return transit.at[pl.ds(column * QUARTER, QUARTER)]
+
+    def x_arrived(k, place):
+        for column in range(1, XS):
+            arrived(place(column), x_recv.at[k, column - 1])
+
+    def pass_on(column):
+        if column:
+            arrived(in_transit(column), x_recv.at[1, column - 1])
+        send(
+            in_transit(column),
+            quarter(1, column),
+            near_send.at[column],
+            near_recv.at[column],
+            device(to_z=z_to[1]),
+        )
 
     for k in (3, 2):
-        send(own_quarter(k), quarter(k, 0), x_send.at[k, 0], x_recv.at[k, 0], device(to_z=z_to[k]))
-    for column, dx in around + ((0, 0),):
-        send(
-            own_quarter(1),
-            quarter(1, column),
-            x_send.at[1, column],
-            x_recv.at[1, column],
-            device(dx=dx, to_z=z_to[1]),
-        )
-    x_spread(0)
+        at = pl.ds(pl.multiple_of(own_at + quarters[k] * QUARTER, QUARTER), QUARTER)
+        send(ui.at[at], quarter(k, 0), z_send.at[k - 1], z_recv.at[k - 1], device(to_z=z_to[k]))
+    x_spread(1, in_transit)
+    pass_on(0)
+    x_spread(0, functools.partial(quarter, 0))
     rows_of = ui.at[own_rows]
     send(rows_of, rows_of, row_send.at[0], row_recv.at[0], device(dc=1))
-    send(rows_of, rows_of, row_send.at[1], row_recv.at[1], device(to_z=z_pair))
+    near_rows = ui.at[pl.ds(pl.multiple_of(own_at + y * QUARTER, QUARTER), QUARTER)]
+    send(near_rows, near_rows, row_send.at[1], row_recv.at[1], device(to_z=z_pair))
     partner_copy.wait()
     unit = ui[own_rows, :]
     node = lax.broadcasted_iota(jnp.int32, (ROWS, ROWS), 0)
@@ -207,53 +224,91 @@
     mate = dot_nn(pairing, unit, HIGHEST)
     mates[...] = mate
     pair_scores[...] = dot_nt(jnp.ones((8, WIDTH), F32), unit * mate, HIGHEST)[0:1]
-    for k in (2, 3):
-        arrived(quarter(k, 0), x_recv.at[k, 0])
-        x_spread(k)
-    arrived(ui.at[pair_rows], row_recv.at[1])
-    rows_of = ui.at[pair_rows]
-    send(rows_of, rows_of, row_send.at[2], row_recv.at[2], device(dc=1))
+    def take(k):
+        arrived(quarter(k, 0), z_recv.at[k - 1])
+        x_spread(k, functools.partial(quarter, k))
+
+    def pair_quarter(dy):
+        at = ((1 - odd) * 2 + core) * ROWS + lax.rem(y + dy, YS) * QUARTER
+        return ui.at[pl.ds(pl.multiple_of(at, QUARTER), QUARTER)]
+
+    def hand_on():
+        arrived(pair_quarter(0), row_recv.at[1])
+        for dy in (2, 1, 3):
+            send(
+                pair_quarter(0),
+                pair_quarter(0),
+                row_send.at[2 + dy],
+                row_recv.at[2 + dy],
+                device(dy=dy),
+            )
+
+    def swap_rows():
+        for dy in (1, 2, 3):
+            arrived(pair_quarter(YS - dy), row_recv.at[2 + dy])
+        rows_of = ui.at[pair_rows]
+        send(rows_of, rows_of, row_send.at[2], row_recv.at[2], device(dc=1))
+
+    hand_on()
+    pass_on(1)
+    pass_on(2)
+    take(2)
+    take(3)
+    pass_on(3)
+    swap_rows()
     arrived(ui.at[sib_rows], row_recv.at[0])
-    arrived(ui.at[last_rows], row_recv.at[2])
-
-    def scores(start, stop):
+
+    def columns_in(start, stop):
         high, low = split(uj[start:stop, :])
         for i, value in enumerate((high, high, low)):
             uj_wide[start:stop, i * WIDTH : (i + 1) * WIDTH] = value
             half = ALL // 2
             at = i * half + start % half
             uj_tall[start // half, at : at + stop - start, :] = value
-        score = dot_nt(ui_wide[...], uj_wide[start:stop, :])
+
+    def scores(start, stop, b):
+        rows = pl.ds(pl.multiple_of(b * 2 * ROWS, 2 * ROWS), 2 * ROWS)
+        score = dot_nt(ui_wide[rows, :], uj_wide[start:stop, :])
         weight = jnp.exp2(score * EXP_SCALE - EXP_SCALE)
         if start == 0:
             col = lax.broadcasted_iota(jnp.int32, (1, stop), 1)
-            diagonal = jnp.where(col < QUARTER, col + own_at + quarters[0] * QUARTER, 4 * ALL)
+            first_row = own_at - b * 2 * ROWS + quarters[0] * QUARTER
+            diagonal = jnp.where(col < QUARTER, col + first_row, 4 * ALL)
             row = lax.broadcasted_iota(jnp.int32, weight.shape, 0)
             weight = jnp.where(row == diagonal, 0.0, weight)
-        weights[:, start:stop] = weight
+        weights[rows, start:stop] = weight
         tiles = [weight[:, i : i + TILE] for i in range(0, stop - start, TILE)]
         part = tiles[0]
         for tile in tiles[1:]:
             part = part + tile
         if start == 0:
-            acc[...] = part
+            acc[rows, :] = part
         else:
-            acc[...] += part
-
-    high, low = split(ui[...])
-    for i, value in enumerate((high, low, high)):
-        ui_wide[:, i * WIDTH : (i + 1) * WIDTH] = value
-    def await_columns(k, start):
-        for column in range(start, XS):
-            arrived(quarter(k, column), x_recv.at[k, column])
-
-    await_columns(0, 1)
-    await_columns(1, 0)
-    scores(0, 384)
-    await_columns(2, 1)
-    scores(384, 512)
-    await_columns(3, 1)
-    scores(512, 768)
+            acc[rows, :] += part
+
+    def rows_in(b):
+        rows = pl.ds(pl.multiple_of(b * 2 * ROWS, 2 * ROWS), 2 * ROWS)
+        high, low = split(ui[rows, :])
+        for i, value in enumerate((high, low, high)):
+            ui_wide[rows, i * WIDTH : (i + 1) * WIDTH] = value
+
+    rows_in(odd)
+    x_arrived(0, functools.partial(quarter, 0))
+    x_arrived(2, functools.partial(quarter, 2))
+    columns_in(0, 384)
+    scores(0, 384, odd)
+    arrived(ui.at[last_rows], row_recv.at[2])
+    rows_in(1 - odd)
+    scores(0, 384, 1 - odd)
+    for column in range(XS):
+        arrived(quarter(1, column), near_recv.at[column])
+    columns_in(384, 512)
+    for b in (odd, 1 - odd):
+        scores(384, 512, b)
+    x_arrived(3, functools.partial(quarter, 3))
+    columns_in(512, 768)
+    for b in (odd, 1 - odd):
+        scores(512, 768, b)
 
     gather_sent = list(sent)
     sent.clear()
@@ -282,7 +337,7 @@
         total = total + sums[i]
     inverse[...] = 1.0 / total
 
-    own_inverse = inverse[core * 2 + odd]
+    own_inverse = inverse[odd * 2 + core]
     for i in range(4):
         inverse_own[i] = own_inverse[:, i * QUARTER : (i + 1) * QUARTER]
 
@@ -308,7 +363,7 @@
     def take_inverse(part):
         columns = slice(part * ALL // 2, (part + 1) * ALL // 2)
         pieces = []
-        for k in (2 * part, 2 * part + 1):
+        for k in PLACE[2 * part : 2 * part + 2]:
             for column in range(XS):
                 if (k, column) != (0, 0):
                     arrived(inverse_cols.at[k, column], inv_recv.at[k, column])
@@ -327,7 +382,7 @@
         return dot_nn(wide[slot], uj_tall[part])
 
     there = (1 - odd, odd)
-    blocks = [(1 - core) * 2 + b for b in there] + [core * 2 + b for b in there]
+    blocks = [b * 2 + 1 - core for b in there] + [b * 2 + core for b in there]
     take_inverse(0)
     for i, block in enumerate(blocks):
         pull_first[i] = pulls(i, block, 0)
@@ -404,6 +459,7 @@
             pltpu.VMEM((ROWS, WIDTH), F32),
             pltpu.VMEM((1, ROWS), F32),
             pltpu.VMEM((ALL, WIDTH), F32),
+            pltpu.VMEM((ROWS, WIDTH), F32),
             pltpu.VMEM((ALL, 3 * WIDTH), BF16),
             pltpu.VMEM((2, 3 * ALL // 2, WIDTH), BF16),
             pltpu.VMEM((ALL, ALL), F32),
@@ -421,10 +477,14 @@
             pltpu.VMEM((2, ROWS, WIDTH), F32),
             pltpu.VMEM((7, SHARE, WIDTH), F32),
             dma((2,)),
-            dma((4, 4)),
-            dma((4, 4)),
             dma((3,)),
             dma((3,)),
+            dma((4,)),
+            dma((4,)),
+            dma((4, 3)),
+            dma((4, 3)),
+            dma((6,)),
+            dma((6,)),
             dma((15,)),
             dma((16,)),
             dma((4, 4)),

time: 47.8 us -> 47.3 us (0.990)
  Pallas kernels: 46.4 us -> 45.9 us
    pallas_call x1, Pallas kernels: 45.7 us -> 45.2 us  [body(): pl.pallas_call(kernel, out_shape=(jax.ShapeDtypeStruct((1, ROWS), F32), j...]
where the time goes in v5:
time: 47.3 us; the launch traced here: 47.2 us
  Pallas kernels  45.9 us (97%)
  local copies, waits for them, and re-layouts  0.67 us (1%)
  between operations  0.65 us (1%)
    pallas_call x1, Pallas kernels, body(): pl.pallas_call(kernel, out_shape=(jax.ShapeDtypeStruct((1, ROWS), F32), j...  45.2 us

profile of v5, /device:TPU:1, one launch (start us, length us, event | category | flops | bytes accessed | tf_op | source)
XLA Modules:
  0.0 47.2 jit_solution(1464703226248415852)
XLA Ops:
  0.6 0.0 copy-start
  0.6 0.7 %copy-done = s32[192]{0:T(256)S(1)} copy-done((s32[192]{0:T(256)S(1)}, s32[192]{0:T(256)}, u32[]{:S(2)}) %copy-start) | copy-done | bytes 792
  1.3 45.2 %shard_map.41 = (f32[1,192]{1,0:T(1,128)S(1)}, f32[192,256]{1,0:T(8,128)S(1)}) custom-call(f32[192,256]{1,0:T(8,128)} %emb_hbm.1, s32[1,192]{1,0:T(1,128)S(1)} %bitcast.2), custom_call_target="tpu_custom_call" | custom-call | tf_op jit(solution)/shard_map/pallas_call | solution.py:445
  46.5 0.7 %shard_map.42 = (f32[1,192]{1,0:T(1,128)}, f32[192,256]{1,0:T(8,128)}) custom-call(f32[1,192]{1,0:T(1,128)S(1)} %get-tuple-element.6.loss_vmem, f32[192,256]{1,0:T(8,128)S(1)} %get-tuple-element.7.grad_vmem), custom_call_target="tpu_custom_call" | custom-call | tf_op jit(solution)/shard_map/pallas_call | solution.py:513
Async XLA Ops:
  0.6 0.7 %copy-start = (s32[192]{0:T(256)S(1)}, s32[192]{0:T(256)}, u32[]{:S(2)}) copy-start(s32[192]{0:T(256)} %param.3) | copy-start | bytes 2308

commit v6 on v5

--- a/solution.py
+++ b/solution.py
@@ -207,7 +207,7 @@
             device(to_z=z_to[1]),
         )
 
-    for k in (3, 2):
+    for k in (2, 3):
         at = pl.ds(pl.multiple_of(own_at + quarters[k] * QUARTER, QUARTER), QUARTER)
         send(ui.at[at], quarter(k, 0), z_send.at[k - 1], z_recv.at[k - 1], device(to_z=z_to[k]))
     x_spread(1, in_transit)
@@ -391,7 +391,6 @@
     for i in range(2):
         pull_out[i] = pull_first[i] + pulls(i, blocks[i], 1)
         send(pull_out.at[i], pull_in.at[i], sib_send.at[i], sib_recv.at[i], device(dc=1))
-    for i in range(2):
         pull_own[i] = pull_first[2 + i] + pulls(2 + i, blocks[2 + i], 1)
 
     def share(at):

time: 47.3 us -> 47.2 us (level)
  no operation moved by 1% of the time
where the time goes in v6:
time: 47.2 us; the launch traced here: 47.1 us
  Pallas kernels  45.7 us (97%)
  local copies, waits for them, and re-layouts  0.67 us (1%)
  between operations  0.65 us (1%)
    pallas_call x1, Pallas kernels, body(): pl.pallas_call(kernel, out_shape=(jax.ShapeDtypeStruct((1, ROWS), F32), j...  45 us

profile of v6, /device:TPU:1, one launch (start us, length us, event | category | flops | bytes accessed | tf_op | source)
XLA Modules:
  0.0 47.1 jit_solution(8159452103404933249)
XLA Ops:
  0.6 0.0 copy-start
  0.6 0.7 %copy-done = s32[192]{0:T(256)S(1)} copy-done((s32[192]{0:T(256)S(1)}, s32[192]{0:T(256)}, u32[]{:S(2)}) %copy-start) | copy-done | bytes 792
  1.3 45.0 %shard_map.41 = (f32[1,192]{1,0:T(1,128)S(1)}, f32[192,256]{1,0:T(8,128)S(1)}) custom-call(f32[192,256]{1,0:T(8,128)} %emb_hbm.1, s32[1,192]{1,0:T(1,128)S(1)} %bitcast.2), custom_call_target="tpu_custom_call" | custom-call | tf_op jit(solution)/shard_map/pallas_call | solution.py:444
  46.4 0.7 %shard_map.42 = (f32[1,192]{1,0:T(1,128)}, f32[192,256]{1,0:T(8,128)}) custom-call(f32[1,192]{1,0:T(1,128)S(1)} %get-tuple-element.6.loss_vmem, f32[192,256]{1,0:T(8,128)S(1)} %get-tuple-element.7.grad_vmem), custom_call_target="tpu_custom_call" | custom-call | tf_op jit(solution)/shard_map/pallas_call | solution.py:512
Async XLA Ops:
  0.6 0.7 %copy-start = (s32[192]{0:T(256)S(1)}, s32[192]{0:T(256)}, u32[]{:S(2)}) copy-start(s32[192]{0:T(256)} %param.3) | copy-start | bytes 2308

commit v7 on v5

--- a/solution.py
+++ b/solution.py
@@ -250,9 +250,9 @@
         send(rows_of, rows_of, row_send.at[2], row_recv.at[2], device(dc=1))
 
     hand_on()
+    take(2)
     pass_on(1)
     pass_on(2)
-    take(2)
     take(3)
     pass_on(3)
     swap_rows()

time: 47.3 us -> 47.3 us (level)
  no operation moved by 1% of the time
where the time goes in v7:
time: 47.3 us; the launch traced here: 47.2 us
  Pallas kernels  45.9 us (97%)
  local copies, waits for them, and re-layouts  0.67 us (1%)
  between operations  0.65 us (1%)
    pallas_call x1, Pallas kernels, body(): pl.pallas_call(kernel, out_shape=(jax.ShapeDtypeStruct((1, ROWS), F32), j...  45.2 us

profile of v7, /device:TPU:1, one launch (start us, length us, event | category | flops | bytes accessed | tf_op | source)
XLA Modules:
  0.0 47.2 jit_solution(7624257626843948285)
XLA Ops:
  0.6 0.0 copy-start
  0.6 0.7 %copy-done = s32[192]{0:T(256)S(1)} copy-done((s32[192]{0:T(256)S(1)}, s32[192]{0:T(256)}, u32[]{:S(2)}) %copy-start) | copy-done | bytes 792
  1.3 45.2 %shard_map.41 = (f32[1,192]{1,0:T(1,128)S(1)}, f32[192,256]{1,0:T(8,128)S(1)}) custom-call(f32[192,256]{1,0:T(8,128)} %emb_hbm.1, s32[1,192]{1,0:T(1,128)S(1)} %bitcast.2), custom_call_target="tpu_custom_call" | custom-call | tf_op jit(solution)/shard_map/pallas_call | solution.py:445
  46.5 0.7 %shard_map.42 = (f32[1,192]{1,0:T(1,128)}, f32[192,256]{1,0:T(8,128)}) custom-call(f32[1,192]{1,0:T(1,128)S(1)} %get-tuple-element.6.loss_vmem, f32[192,256]{1,0:T(8,128)S(1)} %get-tuple-element.7.grad_vmem), custom_call_target="tpu_custom_call" | custom-call | tf_op jit(solution)/shard_map/pallas_call | solution.py:513
Async XLA Ops:
  0.6 0.7 %copy-start = (s32[192]{0:T(256)S(1)}, s32[192]{0:T(256)}, u32[]{:S(2)}) copy-start(s32[192]{0:T(256)} %param.3) | copy-start | bytes 2308
